TPU v7x, 128 devices: a whole 4x4x4 slice. The times are simulated.
128 devices in a mesh: row: 8 (over z, x_lo), col: 16 (over x_hi, y, core).
Axes of the slice: x: 4 (x_hi: 2, x_lo: 2; x = x_hi * 2 + x_lo), y: 4, z: 4, core: 2. Of those that a mesh axis runs over, the one named last changes fastest.
Arguments:
- object_tile: float32 [2, 4096, 8192], P(None, 'row', 'col'), may hold values from -6 to 6
- probe: float32 [2, 256, 256], replicated, may hold values from -6 to 6
- amplitudes: float32 [8, 16, 16, 256, 256], P('row', 'col'), may hold values from 0 to 3
- positions: int32 [8, 16, 16, 2], P('row', 'col'), may hold values from 0 to 511, as said below
- counts: int32 [8, 16], P('row'), may hold values from 0 to 16, as said below
Outputs:
- object_grad: float32 [2, 4096, 8192], P(None, 'row', 'col')
- probe_grad: float32 [2, 256, 256], replicated
Inputs may be any that keep to these rules, and one draw needn't show every extreme that they name: `positions`: offsets place every window inside the object: on the last row index of devices the row offset is at most 256, and on the last column index the column offset at most 256. Over each row index of devices the counts sum to exactly 128.
All inputs are finite; a program needn't handle non-finite values.
Results may differ from a plain program's by a relative error of at most 0.00014.
Values sent between devices are 32-bit elements; how exact they have to be, the bound alone decides.
A program may use at most 192 MiB of HBM per device.

v0:
```python
import math

import jax
import jax.numpy as jnp
from jax import lax
from jax.sharding import PartitionSpec as P

smooth_term = 0.01
highest = lax.Precision.HIGHEST


def from_behind(value, axis, steps):
    count = lax.axis_size(axis)
    initial, last = (max(0, -steps), min(count, count - steps))
    return lax.ppermute(value, axis, [(source, source + steps) for source in range(initial, last)])


def from_row(block, offset):
    return from_behind(block, "row", offset)


def from_col(block, offset):
    return from_behind(block, "col", offset)


def dft_tables(width):
    index = jnp.arange(width, dtype=jnp.int32)
    phase = (index[:, None] * index[None, :] % width).astype(jnp.float32) * (2.0 * math.pi / width)
    factor = 1.0 / math.sqrt(width)
    return (jnp.cos(phase) * factor, -jnp.sin(phase) * factor)


def both_sides(real_part, imag_part, table_re, table_im):
    left_re = jnp.einsum("jk,skl->sjl", table_re, real_part, precision=highest) - jnp.einsum(
        "jk,skl->sjl", table_im, imag_part, precision=highest
    )
    left_im = jnp.einsum("jk,skl->sjl", table_re, imag_part, precision=highest) + jnp.einsum(
        "jk,skl->sjl", table_im, real_part, precision=highest
    )
    right_re = jnp.einsum("sjk,kl->sjl", left_re, table_re, precision=highest) - jnp.einsum(
        "sjk,kl->sjl", left_im, table_im, precision=highest
    )
    right_im = jnp.einsum("sjk,kl->sjl", left_re, table_im, precision=highest) + jnp.einsum(
        "sjk,kl->sjl", left_im, table_re, precision=highest
    )
    return (right_re, right_im)


def slot_terms(windows, probe, amps, live):
    table_re, table_im = dft_tables(probe.shape[1])
    win_re = windows[:, 0]
    win_im = windows[:, 1]
    exit_re = probe[0] * win_re - probe[1] * win_im
    exit_im = probe[0] * win_im + probe[1] * win_re
    wave_re, wave_im = both_sides(exit_re, exit_im, table_re, table_im)
    model = jnp.sqrt(wave_re * wave_re + wave_im * wave_im + smooth_term)
    factor = 2.0 * (1.0 - amps / model) * live[:, None, None]
    back_re, back_im = both_sides(factor * wave_re, factor * wave_im, table_re, -table_im)
    obj_terms = jnp.stack(
        [probe[0] * back_re + probe[1] * back_im, probe[0] * back_im - probe[1] * back_re], axis=1
    )
    probe_re = jnp.sum(win_re * back_re + win_im * back_im, axis=0)
    probe_im = jnp.sum(win_re * back_im - win_im * back_re, axis=0)
    return (obj_terms, jnp.stack([probe_re, probe_im]))


def extend(tile, width):
    below = from_row(tile[:, :width, :], -1)
    tall = jnp.concatenate([tile, below], axis=1)
    right = from_col(tall[:, :, :width], -1)
    return jnp.concatenate([tall, right], axis=2)


def fold(grad_ext, rows, cols, width):
    arrived_rows = from_row(grad_ext[:, rows:, :], 1)
    short = grad_ext[:, :rows, :].at[:, :width, :].add(arrived_rows)
    arrived = from_col(short[:, :, cols:], 1)
    return short[:, :, :cols].at[:, :, :width].add(arrived)


def on_device(object_tile, probe, amplitudes, positions, counts):
    rows = object_tile.shape[1]
    cols = object_tile.shape[2]
    width = probe.shape[1]
    extended = extend(object_tile, width)
    own_pos = positions[0, 0]
    capacity = own_pos.shape[0]
    line = counts[0]
    my_col = lax.axis_index("col")
    mine = lax.dynamic_index_in_dim(line, my_col, 0, keepdims=False)
    slot_ids = jnp.arange(capacity, dtype=jnp.int32)
    live = slot_ids < mine
    zero = jnp.int32(0)

    def cut_window(offset):
        return lax.dynamic_slice(extended, (zero, offset[0], offset[1]), (2, width, width))

    windows = jax.vmap(cut_window)(own_pos)
    amps = amplitudes[0, 0]
    obj_terms, probe_part = slot_terms(windows, probe, amps, live.astype(jnp.float32))

    def add_window(index, grad_ext):
        offset = own_pos[index]
        current = lax.dynamic_slice(grad_ext, (zero, offset[0], offset[1]), (2, width, width))
        return lax.dynamic_update_slice(
            grad_ext, current + obj_terms[index], (zero, offset[0], offset[1])
        )

    grad_ext = lax.fori_loop(0, capacity, add_window, jnp.zeros_like(extended))
    probe_grad = lax.psum(probe_part, ("row", "col"))
    object_grad = fold(grad_ext, rows, cols, width)
    return (object_grad, probe_grad)


def solution(mesh):
    in_specs = (
        P(None, "row", "col"),
        P(),
        P("row", "col", None, None, None),
        P("row", "col", None, None),
        P("row", None),
    )
    out_specs = (P(None, "row", "col"), P())
    return jax.shard_map(
        on_device, mesh=mesh, in_specs=in_specs, out_specs=out_specs, check_vma=False
    )
```

profile of v0, /device:TPU:1, one launch (start us, length us, event | category | flops | bytes accessed | tf_op | source)
XLA Modules:
  0.0 697.9 jit_solution(758928300086582022)
XLA Ops:
  11.6 23.3 %collective-permute-done = f32[2,256,512]{2,1,0:T(8,128)S(1)} collective-permute-done((f32[2,256,512]{2,1,0:T(8,128)S(1)}, f32[2,256,512]{2,1,0:T(8,128)S(1)}, u32[]{:S(2)}, u32[]{:S(2)}) %collective-permute-start) | collective-permute-done | bytes 1048608 | tf_op jit(solution)/shard_map/ppermute | solution.py:15
  36.2 3.6 collective-permute-start.1
  43.0 16.7 %collective-permute-done.1 = f32[2,768,256]{2,1,0:T(8,128)} collective-permute-done((f32[2,768,256]{2,1,0:T(8,128)}, f32[2,768,256]{2,1,0:T(8,128)}, u32[]{:S(2)}, u32[]{:S(2)}) %collective-permute-start.1) | collective-permute-done | bytes 1572896 | tf_op jit(solution)/shard_map/ppermute | solution.py:15
  59.7 4.0 pad_maximum_fusion.1
  63.7 63.5 %while.17 = (s32[]{:T(128)}, f32[2,768,768]{2,1,0:T(8,128)}, s32[16,3]{0,1:T(4,128)S(1)}, f32[16,2,256,256]{3,2,0,1:T(8,128)}, s32[]{:T(128)}) while((s32[]{:T(128)}, f32[2,768,768]{2,1,0:T(8,128)}, s32[16,3]{0,1:T(4,128)S(1)}, f32[16,2,256,256]{3,2,0,1:T(8,128)}, s32[]{:T(128)}) %tuple.65), condition=%wide.while_cond.2, body=%wide.while_body.2.sunk | while | flops 2 | bytes 1050217 | solution.py:96
  72.2 3.4 bitcast_dynamic-update-slice_fusion.2
  80.2 3.4 bitcast_dynamic-update-slice_fusion.2
  107.9 3.4 bitcast_dynamic-update-slice_fusion.2
  123.8 3.4 bitcast_dynamic-update-slice_fusion.2
  127.2 11.7 %fusion.43 = f32[16,256,256]{2,1,0:T(8,128)S(1)} fusion(f32[16,2,256,256]{3,2,0,1:T(8,128)} %get-tuple-element.113, f32[256,256]{1,0:T(8,128)S(1)} %copy-done.4, f32[256,256]{1,0:T(8,128)S(1)} %get-tuple-element.146), kind=kOutput, calls=%fused_computation.55 | convolution fusion | flops 3225354240 | bytes 13107200 | tf_op jit(solution)/shard_map/jk,skl->sjl/dot_general | solution.py:34
  138.9 8.3 %fusion.39 = f32[16,256,256]{2,1,0:T(8,128)S(1)} fusion(f32[16,2,256,256]{3,2,0,1:T(8,128)S(1)} %copy-done.2, f32[256,256]{1,0:T(8,128)S(1)} %copy-done.4, f32[256,256]{1,0:T(8,128)S(1)} %get-tuple-element.146), kind=kOutput, calls=%fused_computation.54 | convolution fusion | flops 3225354240 | bytes 13107200 | tf_op jit(solution)/shard_map/jk,skl->sjl/dot_general | solution.py:37
  147.2 8.8 %convolution_add_fusion.1 = f32[16,256,256]{2,1,0:T(8,128)S(1)} fusion(f32[16,256,256]{2,1,0:T(8,128)S(1)} %fusion.39, f32[16,2,256,256]{3,2,0,1:T(8,128)S(1)} %copy-done.2, f32[256,256]{1,0:T(8,128)S(1)} %copy-done.4, f32[256,256]{1,0:T(8,128)S(1)} %get-tuple-element.146), kind=kOutput, calls=%fused_computation.49 | convolution fusion | flops 3226468352 | bytes 17301504 | tf_op jit(solution)/shard_map/jk,skl->sjl/dot_general | solution.py:37
  156.1 8.0 %fusion.8 = f32[16,256,256]{2,1,0:T(8,128)S(1)} fusion(f32[16,256,256]{2,1,0:T(8,128)S(1)} %convolution_add_fusion.1), kind=kOutput, calls=%fused_computation.14 | convolution fusion | flops 3222208512 | bytes 8388608 | tf_op jit(solution)/shard_map/sjk,kl->sjl/dot_general | solution.py:43
  164.0 10.4 %fusion.10 = f32[16,256,256]{2,1,0:T(8,128)} fusion(f32[16,256,256]{2,1,0:T(8,128)S(1)} %convolution_add_fusion.1), kind=kOutput, calls=%fused_computation.16 | convolution fusion | flops 3222274048 | bytes 8388608 | tf_op jit(solution)/shard_map/sjk,kl->sjl/dot_general | solution.py:40
  174.4 8.4 %convolution_subtract_fusion.1 = f32[16,256,256]{2,1,0:T(8,128)S(1)} fusion(f32[16,256,256]{2,1,0:T(8,128)S(1)} %fusion.43, f32[16,2,256,256]{3,2,0,1:T(8,128)S(1)} %copy-done.2, f32[256,256]{1,0:T(8,128)S(1)} %copy-done.4, f32[256,256]{1,0:T(8,128)S(1)} %get-tuple-element.146), kind=kOutput, calls=%fused_computation.50 | convolution fusion | flops 3226468352 | bytes 17301504 | tf_op jit(solution)/shard_map/jk,skl->sjl/dot_general | solution.py:34
  182.8 8.2 %fusion.29 = f32[16,256,256]{2,1,0:T(8,128)S(1)} fusion(f32[16,256,256]{2,1,0:T(8,128)S(1)} %fusion.8, f32[16,256,256]{2,1,0:T(8,128)S(1)} %convolution_subtract_fusion.1), kind=kOutput, calls=%fused_computation.44 | convolution fusion | flops 3223322624 | bytes 12582912 | tf_op jit(solution)/shard_map/sjk,kl->sjl/dot_general | solution.py:43
  191.1 13.8 %fusion.25 = (f32[16,256,256]{2,1,0:T(8,128)S(1)}, f32[16,256,256]{2,1,0:T(8,128)S(1)}) fusion(f32[1,1,16,256,256]{4,3,2,1,0:T(8,128)} %param.13, f32[16,256,256]{2,1,0:T(8,128)S(1)} %fusion.29, f32[16]{0:T(128)S(1)} %compare_select_fusion.2, f32[16,256,256]{2,1,0:T(8,128)} %fusion.10, f32[16,256,256]{2,1,0:T(8,128)S(1)} %convolution_subtract_fusion.1), kind=kOutput, calls=%fused_computation.42 | convolution fusion | flops 3232694272 | bytes 25165888 | tf_op jit(solution)/shard_map/sjk,kl->sjl/dot_general | solution.py:40
  204.8 8.3 %fusion.60 = f32[16,256,256]{2,1,0:T(8,128)S(1)} fusion(f32[16,256,256]{2,1,0:T(8,128)S(1)} %get-tuple-element.140), kind=kOutput, calls=%fused_computation.75 | convolution fusion | flops 3222208512 | bytes 8388608 | tf_op jit(solution)/shard_map/jk,skl->sjl/dot_general | solution.py:34
  213.1 8.1 %fusion.57 = f32[16,256,256]{2,1,0:T(8,128)S(1)} fusion(f32[16,256,256]{2,1,0:T(8,128)S(1)} %get-tuple-element.141), kind=kOutput, calls=%fused_computation.72 | convolution fusion | flops 3222208512 | bytes 8388608 | tf_op jit(solution)/shard_map/jk,skl->sjl/dot_general | solution.py:37
  221.2 8.3 %convolution_add_fusion = f32[16,256,256]{2,1,0:T(8,128)S(1)} fusion(f32[16,256,256]{2,1,0:T(8,128)S(1)} %fusion.57, f32[16,256,256]{2,1,0:T(8,128)S(1)} %get-tuple-element.140), kind=kOutput, calls=%fused_computation.47 | convolution fusion | flops 3223388160 | bytes 12582912 | tf_op jit(solution)/shard_map/jk,skl->sjl/dot_general | solution.py:37
  229.6 8.2 %fusion = f32[16,256,256]{2,1,0:T(8,128)S(1)} fusion(f32[16,256,256]{2,1,0:T(8,128)S(1)} %convolution_add_fusion), kind=kOutput, calls=%fused_computation.6 | convolution fusion | flops 3222208512 | bytes 8388608 | tf_op jit(solution)/shard_map/sjk,kl->sjl/dot_general | solution.py:43
  237.8 8.8 %fusion.2 = f32[16,256,256]{2,1,0:T(8,128)S(1)} fusion(f32[16,256,256]{2,1,0:T(8,128)S(1)} %convolution_add_fusion), kind=kOutput, calls=%fused_computation.8 | convolution fusion | flops 3222339584 | bytes 8388608 | tf_op jit(solution)/shard_map/sjk,kl->sjl/dot_general | solution.py:40
  246.6 8.4 %convolution_subtract_fusion = f32[16,256,256]{2,1,0:T(8,128)S(1)} fusion(f32[16,256,256]{2,1,0:T(8,128)S(1)} %fusion.60, f32[16,256,256]{2,1,0:T(8,128)S(1)} %get-tuple-element.141), kind=kOutput, calls=%fused_computation.48 | convolution fusion | flops 3223388160 | bytes 12582912 | tf_op jit(solution)/shard_map/jk,skl->sjl/dot_general | solution.py:34
  255.0 8.3 %fusion.35 = f32[16,256,256]{2,1,0:T(8,128)S(1)} fusion(f32[16,256,256]{2,1,0:T(8,128)S(1)} %fusion, f32[16,256,256]{2,1,0:T(8,128)S(1)} %convolution_subtract_fusion), kind=kOutput, calls=%fused_computation.46 | convolution fusion | flops 3223388160 | bytes 12582912 | tf_op jit(solution)/shard_map/sjk,kl->sjl/dot_general | solution.py:43
  263.3 16.0 %fusion.19 = (f32[256,256]{1,0:T(8,128)}, f32[256,256]{1,0:T(8,128)}, f32[16,1,256,256]{3,2,0,1:T(8,128)}, f32[16,1,256,256]{3,2,0,1:T(8,128)}) fusion(f32[16,256,256]{2,1,0:T(8,128)S(1)} %fusion.35, f32[16,2,256,256]{3,2,0,1:T(8,128)S(1)} %copy-done.2, f32[256,256]{1,0:T(8,128)} %get-tuple-element.147, f32[256,256]{1,0:T(8,128)} %copy-done.3, ...), kind=kOutput, calls=%fused_computation.29 | convolution fusion | flops 3237806080 | bytes 30408704 | tf_op jit(solution)/shard_map/sjk,kl->sjl/dot_general | solution.py:40
  279.4 7.6 %pad_maximum_fusion = f32[16,2,256,256]{3,2,0,1:T(8,128)} fusion(f32[16,1,256,256]{3,2,0,1:T(8,128)} %get-tuple-element.144, f32[16,1,256,256]{3,2,0,1:T(8,128)} %get-tuple-element.145), kind=kLoop, calls=%fused_computation.4 | loop fusion | flops 2097152 | bytes 16777216 | tf_op jit(solution)/shard_map/stack | solution.py:59
  289.4 205.9 %while.16 = (s32[]{:T(128)}, f32[2,768,768]{2,1,0:T(8,128)}, s32[16,2]{0,1:T(2,128)S(1)}, f32[16,2,256,256]{3,2,0,1:T(8,128)}, s32[]{:T(128)}, /*index=5*/s32[]{:T(128)}, s32[]{:T(128)}) while((s32[]{:T(128)}, f32[2,768,768]{2,1,0:T(8,128)}, s32[16,2]{0,1:T(2,128)S(1)}, f32[16,2,256,256]{3,2,0,1:T(8,128)}, s32[]{:T(128)}, ...), condition=%wide.region_1.2_spmd, body=%wide.region_0.1_spmd.sunk | while | flops 131080 | bytes 2621637 | solution.py:109
  295.6 6.8 dynamic_update_slice.8
  308.6 6.8 dynamic_update_slice.8
  321.6 6.1 dynamic_update_slice.8
  333.9 6.8 dynamic_update_slice.8
  346.9 6.6 dynamic_update_slice.8
  359.8 6.5 dynamic_update_slice.8
  372.5 6.2 dynamic_update_slice.8
  385.0 6.8 dynamic_update_slice.8
  398.0 6.8 dynamic_update_slice.8
  411.0 6.8 dynamic_update_slice.8
  424.0 6.6 dynamic_update_slice.8
  436.8 6.7 dynamic_update_slice.8
  449.7 6.8 dynamic_update_slice.8
  462.7 6.8 dynamic_update_slice.8
  475.8 6.6 dynamic_update_slice.8
  488.6 6.8 dynamic_update_slice.8
  496.9 4.0 collective-permute-start.2
  503.0 15.1 %collective-permute-done.2 = f32[2,256,768]{2,1,0:T(8,128)S(1)} collective-permute-done((f32[2,256,768]{2,1,0:T(8,128)S(1)}, f32[2,256,768]{2,1,0:T(8,128)S(1)}, u32[]{:S(2)}, u32[]{:S(2)}) %collective-permute-start.2) | collective-permute-done | bytes 1572896 | tf_op jit(solution)/shard_map/ppermute | solution.py:15
  520.8 18.5 %collective-permute-start.3 = (f32[2,512,256]{2,1,0:T(8,128)}, f32[2,512,256]{2,1,0:T(8,128)}, u32[]{:S(2)}, u32[]{:S(2)}) collective-permute-start(f32[2,512,256]{2,1,0:T(8,128)} %slice.142), channel_id=1, source_target_pairs={{0,1},{1,2},{2,3},{3,4},{4,5},{5,6},{6,7},{7,8},{8,9},{9,10},{10,1... | collective-permute-start | bytes 3145736 | tf_op jit(solution)/shard_map/ppermute | solution.py:15
  541.9 9.5 %collective-permute-done.3 = f32[2,512,256]{2,1,0:T(8,128)} collective-permute-done((f32[2,512,256]{2,1,0:T(8,128)}, f32[2,512,256]{2,1,0:T(8,128)}, u32[]{:S(2)}, u32[]{:S(2)}) %collective-permute-start.3) | collective-permute-done | bytes 1048608 | tf_op jit(solution)/shard_map/ppermute | solution.py:15
  553.8 135.1 %all-reduce.2.cloned.1.call-done = f32[2,256,256]{2,1,0:T(8,128)} async-done(((f32[2,256,256]{2,1,0:T(8,128)}), f32[2,256,256]{2,1,0:T(8,128)}) %all-reduce.2.cloned.1.call-update) | async-done | bytes 524304 | tf_op jit(solution)/shard_map/psum | solution.py:110
  (131 shorter events, 109.5 us)
Async XLA Ops:
  7.2 32.7 %copy-start = (s32[1,16]{1,0:T(1,128)S(1)}, s32[1,16]{1,0:T(1,128)}, u32[]{:S(2)}) copy-start(s32[1,16]{1,0:T(1,128)} %param.15) | copy-start | bytes 196
  7.2 681.8 %all-reduce.2.cloned.1.call-start = ((), (), s32[]{:S(2)}) async-start(), calls=%async_computation | async-start | bytes 1048576 | tf_op jit(solution)/shard_map/psum | solution.py:110
  8.5 32.6 %copy-start.7 = (s32[1,1,16,2]{2,3,1,0:T(2,128)S(1)}, s32[1,1,16,2]{2,3,1,0:T(2,128)}, u32[]{:S(2)}) copy-start(s32[1,1,16,2]{2,3,1,0:T(2,128)} %param.14) | copy-start | bytes 388
  8.5 26.3 %collective-permute-start = (f32[2,256,512]{2,1,0:T(8,128)S(1)}, f32[2,256,512]{2,1,0:T(8,128)S(1)}, u32[]{:S(2)}, u32[]{:S(2)}) collective-permute-start(f32[2,256,512]{2,1,0:T(8,128)S(1)} %slice.111), channel_id=1, source_target_pairs={{16,0},{32,16},{48,32},{64,48},{80,64},{96,80},{112,96},{17,1},{33... | collective-permute-start | bytes 3145736 | tf_op jit(solution)/shard_map/ppermute | solution.py:15
  36.2 23.5 %collective-permute-start.1 = (f32[2,768,256]{2,1,0:T(8,128)}, f32[2,768,256]{2,1,0:T(8,128)}, u32[]{:S(2)}, u32[]{:S(2)}) collective-permute-start(f32[2,768,256]{2,1,0:T(8,128)} %slice.139), channel_id=1, source_target_pairs={{1,0},{2,1},{3,2},{4,3},{5,4},{6,5},{7,6},{8,7},{9,8},{10,9},{11,1... | collective-permute-start | bytes 4718600 | tf_op jit(solution)/shard_map/ppermute | solution.py:15
  43.0 131.4 %copy-start.3 = (f32[256,256]{1,0:T(8,128)}, f32[256,256]{1,0:T(8,128)S(1)}, u32[]{:S(2)}) copy-start(f32[256,256]{1,0:T(8,128)S(1)} %get-tuple-element.146) | copy-start | bytes 786436
  63.7 63.5 %copy-start.4 = (f32[256,256]{1,0:T(8,128)S(1)}, f32[256,256]{1,0:T(8,128)}, u32[]{:S(2)}) copy-start(f32[256,256]{1,0:T(8,128)} %get-tuple-element.147) | copy-start | bytes 786436
  127.2 11.7 %copy-start.2 = (f32[16,2,256,256]{3,2,0,1:T(8,128)S(1)}, f32[16,2,256,256]{3,2,0,1:T(8,128)}, u32[]{:S(2)}) copy-start(f32[16,2,256,256]{3,2,0,1:T(8,128)} %get-tuple-element.113) | copy-start | bytes 25165828
  496.9 21.2 %collective-permute-start.2 = (f32[2,256,768]{2,1,0:T(8,128)S(1)}, f32[2,256,768]{2,1,0:T(8,128)S(1)}, u32[]{:S(2)}, u32[]{:S(2)}) collective-permute-start(f32[2,256,768]{2,1,0:T(8,128)S(1)} %slice.120), channel_id=1, source_target_pairs={{0,16},{16,32},{32,48},{48,64},{64,80},{80,96},{96,112},{1,17},{17... | collective-permute-start | bytes 4718600 | tf_op jit(solution)/shard_map/ppermute | solution.py:15
  503.0 36.4 %copy-start.5 = (f32[256,256]{1,0:T(8,128)S(1)}, f32[256,256]{1,0:T(8,128)}, u32[]{:S(2)}) copy-start(f32[256,256]{1,0:T(8,128)} %get-tuple-element.118) | copy-start | bytes 786436
  503.0 36.4 %copy-start.6 = (f32[256,256]{1,0:T(8,128)S(1)}, f32[256,256]{1,0:T(8,128)}, u32[]{:S(2)}) copy-start(f32[256,256]{1,0:T(8,128)} %get-tuple-element.119) | copy-start | bytes 786436
  520.8 30.6 %collective-permute-start.3 = (f32[2,512,256]{2,1,0:T(8,128)}, f32[2,512,256]{2,1,0:T(8,128)}, u32[]{:S(2)}, u32[]{:S(2)}) collective-permute-start(f32[2,512,256]{2,1,0:T(8,128)} %slice.142), channel_id=1, source_target_pairs={{0,1},{1,2},{2,3},{3,4},{4,5},{5,6},{6,7},{7,8},{8,9},{9,10},{10,1... | collective-permute-start | bytes 3145736 | tf_op jit(solution)/shard_map/ppermute | solution.py:15
  540.2 150.6 %copy-start.1 = (s32[1,16]{1,0:T(1,128)S(1)}, s32[1,16]{1,0:T(1,128)}, u32[]{:S(2)}) copy-start(s32[1,16]{1,0:T(1,128)} %param.15) | copy-start | bytes 196
Sparse Core Ops, SparseCore 0:
  540.4 148.5 all-reduce.1
where the time goes:
time: 708 us; the launch traced here: 698 us
  waiting for transfers between devices  200 us (28%)
  local copies, waits for them, and re-layouts  198 us (28%)
  matrix products  152 us (21%)
  loops' own time  64.3 us (9%)
  other arithmetic  41.6 us (6%)
  starting transfers between devices  27.5 us (4%)
  between operations  14.6 us (2%)
    psum x1, waiting for transfers between devices, on_device(): probe_grad = lax.psum(probe_part, ('row', 'col'))  135 us
    dynamic_update_slice x16, local copies, waits for them, and re-layouts, add_window(): lax.dynamic_update_slice(grad_ext, current + obj_terms[index], (zero, off...  106 us
    ppermute x4, waiting for transfers between devices, from_behind(): lax.ppermute(value, axis, [(source, source + steps) for source in range(i...  64.6 us
    another operation x1, loops' own time, on_device(): grad_ext = lax.fori_loop(0, capacity, add_window, jnp.zeros_like(extended))  64.3 us
    gather x48, local copies, waits for them, and re-layouts  63.4 us
    dot_general x2, matrix products, both_sides(): jnp.einsum('sjk,kl->sjl', left_re, table_re, precision=highest)  29.8 us
    ppermute x4, starting transfers between devices, from_behind(): lax.ppermute(value, axis, [(source, source + steps) for source in range(i...  27.4 us
    add x16, other arithmetic, add_window(): current + obj_terms[index]  24.5 us
  transfers between devices with their start and end apart: 5, of which 5 were waited for; matrix products, arithmetic and copies ran while one was open for 2% of the time, Pallas kernels for 0%

commit v1 on v0

v1 whole, which is shorter than its diff:
```python
import functools
import math

import jax
import jax.numpy as jnp
import numpy as np
from jax import lax
from jax.experimental import pallas as pl
from jax.experimental.pallas import tpu as pltpu
from jax.sharding import PartitionSpec as P

smooth_term = 0.01
F32 = jnp.float32
BF16 = jnp.bfloat16
W = 256
H = 128
CH = 32
VMEM = pltpu.VMEM


def split_table(table):
    high = table.astype(jnp.bfloat16)
    low = (table - high.astype(np.float64)).astype(jnp.bfloat16)
    return high, low


def half_tables():
    n = np.arange(H)
    even = np.exp(-2j * np.pi * np.outer(n, n) / H) / 16.0
    odd = np.exp(-2j * np.pi * n / W)[:, None] * even

    def real_form(z):
        return np.block([[z.real, z.imag], [-z.imag, z.real]])

    return real_form(even), real_form(odd), real_form(even.conj().T), real_form(odd.conj().T)


def tables():
    even, odd, inv_even, inv_odd = half_tables()
    right, left = [], []
    for table in (even, odd, inv_even, inv_odd):
        high, low = split_table(table)
        right.append(np.concatenate([high, high, low], axis=0))
        high, low = split_table(table.T)
        left.append(np.concatenate([high, high, low], axis=1))
    return np.stack(right), np.stack(left)


def high_low(value):
    high = value.astype(BF16)
    return high, (value - high.astype(F32)).astype(BF16)


def put_cols(ref, rows, half, value):
    high, low = high_low(value)
    at = H * half
    ref[rows, at : at + H] = high
    ref[rows, W + at : W + at + H] = low
    ref[rows, 2 * W + at : 2 * W + at + H] = high


def put_rows(ref, row, cols, value):
    high, low = high_low(value)
    count = value.shape[0]
    ref[row : row + count, cols] = high
    ref[W + row : W + row + count, cols] = low
    ref[2 * W + row : 2 * W + row + count, cols] = high


def dot(a, b):
    return jnp.dot(a, b, preferred_element_type=F32)


def slot_work(r, c, ext, gext, probe, amp, right_t, left_t, win, xe, xo, ye, yo, ve, vo, pgrad):
    j0 = lax.shift_right_logical(c, 7)
    s = lax.bitwise_and(c, 127)
    back_shift = lax.bitwise_and(128 - s, 127)
    lane = lax.broadcasted_iota(jnp.int32, (CH, H), 1)
    first = lane < 128 - s
    for i in range(W // CH):
        rows = pl.ds(i * CH, CH)
        parts = []
        for p in range(2):
            t = [
                pltpu.roll(ext[p, j0 + q, pl.ds(r + i * CH, CH), :], back_shift, 1)
                for q in range(3)
            ]
            a = jnp.where(first, t[0], t[1])
            b = jnp.where(first, t[1], t[2])
            win[p, rows, 0:H] = a
            win[p, rows, H:W] = b
            parts.append((a, b))
        (are, bre), (aim, bim) = parts
        pra, prb = probe[0, rows, 0:H], probe[0, rows, H:W]
        pia, pib = probe[1, rows, 0:H], probe[1, rows, H:W]
        ea_re = pra * are - pia * aim
        ea_im = pra * aim + pia * are
        eb_re = prb * bre - pib * bim
        eb_im = prb * bim + pib * bre
        put_cols(xe, rows, 0, ea_re + eb_re)
        put_cols(xe, rows, 1, ea_im + eb_im)
        put_cols(xo, rows, 0, ea_re - eb_re)
        put_cols(xo, rows, 1, ea_im - eb_im)
    ye[...] = dot(xe[...], right_t[0])
    yo[...] = dot(xo[...], right_t[1])
    for i in range(H // CH):
        top = pl.ds(i * CH, CH)
        bot = pl.ds(H + i * CH, CH)
        for half, y in ((0, ye), (1, yo)):
            cols = pl.ds(H * half, H)
            for part in range(2):
                t, b = y[top, H * part : H * part + H], y[bot, H * part : H * part + H]
                put_rows(ve, H * part + i * CH, cols, t + b)
                put_rows(vo, H * part + i * CH, cols, t - b)
    ye[...] = dot(left_t[0], ve[...])
    yo[...] = dot(left_t[1], vo[...])
    for i in range(H // CH):
        for half, y, v in ((0, ye, ve), (1, yo, vo)):
            re = y[pl.ds(i * CH, CH), :]
            im = y[pl.ds(H + i * CH, CH), :]
            a = amp[pl.ds(H * half + i * CH, CH), :]
            f = 2.0 - (2.0 * a) * lax.rsqrt(re * re + im * im + smooth_term)
            put_rows(v, i * CH, slice(None), f * re)
            put_rows(v, H + i * CH, slice(None), f * im)
    ye[...] = dot(left_t[2], ve[...])
    yo[...] = dot(left_t[3], vo[...])
    for i in range(H // CH):
        for part in range(2):
            e = ye[pl.ds(H * part + i * CH, CH), :]
            o = yo[pl.ds(H * part + i * CH, CH), :]
            for at, value in ((0, e + o), (H, e - o)):
                rows = pl.ds(at + i * CH, CH)
                put_cols(xe, rows, part, value[:, 0:H])
                put_cols(xo, rows, part, value[:, H:W])
    ye[...] = dot(xe[...], right_t[2])
    yo[...] = dot(xo[...], right_t[3])
    later = lane >= s
    for i in range(W // CH):
        rows = pl.ds(i * CH, CH)
        e_re, e_im = ye[rows, 0:H], ye[rows, H:W]
        o_re, o_im = yo[rows, 0:H], yo[rows, H:W]
        terms = []
        for cols, b_re, b_im in ((slice(0, H), e_re + o_re, e_im + o_im), (slice(H, W), e_re - o_re, e_im - o_im)):
            pr, pi = probe[0, rows, cols], probe[1, rows, cols]
            wr, wi = win[0, rows, cols], win[1, rows, cols]
            at = cols.start * 2 + i * CH
            pgrad[at : at + CH, :] += wr * b_re + wi * b_im
            pgrad[2 * W + at : 2 * W + at + CH, :] += wr * b_im - wi * b_re
            terms.append((pr * b_re + pi * b_im, pr * b_im - pi * b_re))
        for p in range(2):
            ra = pltpu.roll(terms[0][p], s, 1)
            rb = pltpu.roll(terms[1][p], s, 1)
            at = pl.ds(r + i * CH, CH)
            gext[p, j0, at, :] += jnp.where(later, ra, 0.0)
            gext[p, j0 + 1, at, :] += jnp.where(later, rb, ra)
            gext[p, j0 + 2, at, :] += jnp.where(later, 0.0, rb)


def slots_kernel(
    pos, cnt, tile, right, below_l, below_r, corner, amps, probe, right_t, left_t,
    g_tile, g_right, g_below_l, g_below_r, g_corner, pgrad,
    ext, gext, amp_buf, win, xe, xo, ye, yo, ve, vo, in_sem, amp_sem, out_sem,
):
    def pieces(arrays, buf):
        t, rt, bl, br, cn = arrays
        out = []
        for j in range(4):
            out.append((t.at[:, :, pl.ds(H * j, H)], buf.at[:, j, pl.ds(0, 512), :]))
        for j in range(2):
            cols = pl.ds(H * j, H)
            out.append((rt.at[:, :, cols], buf.at[:, 4 + j, pl.ds(0, 512), :]))
            out.append((bl.at[:, :, cols], buf.at[:, j, pl.ds(512, 256), :]))
            out.append((br.at[:, :, cols], buf.at[:, 2 + j, pl.ds(512, 256), :]))
            out.append((cn.at[:, :, cols], buf.at[:, 4 + j, pl.ds(512, 256), :]))
        return out

    def amp_copy(k, slot):
        return pltpu.make_async_copy(amps.at[k], amp_buf.at[slot], amp_sem.at[slot])

    loads = [
        pltpu.make_async_copy(hbm, vm, in_sem.at[n])
        for n, (hbm, vm) in enumerate(pieces((tile, right, below_l, below_r, corner), ext))
    ]
    for copy in loads:
        copy.start()
    count = cnt[0]

    @pl.when(count > 0)
    def _():
        amp_copy(0, 0).start()

    gext[...] = jnp.zeros_like(gext)
    pgrad[...] = jnp.zeros_like(pgrad)
    for copy in loads:
        copy.wait()

    def body(k, _):
        slot = lax.bitwise_and(k, 1)

        @pl.when(k + 1 < count)
        def _():
            amp_copy(k + 1, 1 - slot).start()

        amp_copy(k, slot).wait()
        slot_work(
            pos[k, 0], pos[k, 1], ext, gext, probe, amp_buf.at[slot], right_t, left_t,
            win, xe, xo, ye, yo, ve, vo, pgrad,
        )
        return 0

    lax.fori_loop(0, count, body, 0)
    stores = [
        pltpu.make_async_copy(vm, hbm, out_sem.at[n])
        for n, (hbm, vm) in enumerate(pieces((g_tile, g_right, g_below_l, g_below_r, g_corner), gext))
    ]
    for copy in stores:
        copy.start()
    for copy in stores:
        copy.wait()


def run_slots(own_pos, count, tile, right, below_l, below_r, corner, amps, probe):
    right_t, left_t = tables()
    any_spec = pl.BlockSpec(memory_space=pl.ANY)
    vmem = pl.BlockSpec(memory_space=pltpu.VMEM)
    smem = pl.BlockSpec(memory_space=pltpu.SMEM)
    block = lambda *shape: jax.ShapeDtypeStruct(shape, F32)
    return pl.pallas_call(
        slots_kernel,
        out_shape=(
            block(2, 512, 512), block(2, 512, 256), block(2, 256, 256), block(2, 256, 256),
            block(2, 256, 256), block(4 * W, H),
        ),
        in_specs=[smem, smem] + [any_spec] * 6 + [vmem] * 3,
        out_specs=tuple([any_spec] * 5 + [vmem]),
        scratch_shapes=[
            VMEM((2, 6, 768, H), F32),
            VMEM((2, 6, 768, H), F32),
            VMEM((2, W, W), F32),
            VMEM((2, W, W), F32),
            VMEM((W, 3 * W), BF16),
            VMEM((W, 3 * W), BF16),
            VMEM((W, W), F32),
            VMEM((W, W), F32),
            VMEM((3 * W, W), BF16),
            VMEM((3 * W, W), BF16),
            pltpu.SemaphoreType.DMA((12,)),
            pltpu.SemaphoreType.DMA((2,)),
            pltpu.SemaphoreType.DMA((12,)),
        ],
        compiler_params=pltpu.CompilerParams(vmem_limit_bytes=48 * 1024 * 1024),
        name="slots",
    )(own_pos, count, tile, right, below_l, below_r, corner, amps, probe, jnp.asarray(right_t), jnp.asarray(left_t))


def reorder_kernel(amp_l, amp_r, select_t, amp_out):
    half = jnp.concatenate(
        [
            jnp.concatenate([ref[0, pl.ds(start, H, stride=2), :] for ref in (amp_l, amp_r)], axis=1)
            for start in range(2)
        ],
        axis=0,
    )
    amp_out[0] = jnp.dot(half, select_t[...], precision=lax.Precision.HIGHEST, preferred_element_type=F32)


def reorder(amps):
    n = np.arange(H)
    select = np.zeros((W, W), np.float32)
    select[2 * n, n] = 1.0
    select[2 * n + 1, H + n] = 1.0
    return pl.pallas_call(
        reorder_kernel,
        grid=(amps.shape[0],),
        out_shape=jax.ShapeDtypeStruct(amps.shape, F32),
        in_specs=[
            pl.BlockSpec((1, W, H), lambda k: (k, 0, 0)),
            pl.BlockSpec((1, W, H), lambda k: (k, 0, 1)),
            pl.BlockSpec((W, W), lambda k: (0, 0)),
        ],
        out_specs=pl.BlockSpec((1, W, W), lambda k: (k, 0, 0)),
        name="reorder",
    )(amps, amps, jnp.asarray(select))


MESH = pl.DeviceIdType.MESH


def total_kernel(part, out, full, got0, acc0, got1, acc1, got2, s_send, s_recv, z_send, z_recv, n_send, n_recv):
    row, col = lax.axis_index("row"), lax.axis_index("col")
    z, x_lo = row // 2, row % 2
    x_hi, y, core = col // 8, (col // 2) % 4, col % 2
    plane = (x_hi * 2 + x_lo) * 4 + y

    mate = (row, col + 1 - 2 * core)

    def z_peer(q):
        return (z + q) % 4

    def z_id(q):
        return (z_peer(q) * 2 + x_lo, col)

    def plane_peer(q):
        return (plane + q) % 16

    def plane_id(q):
        n = plane_peer(q)
        x = n // 4
        return (z * 2 + x % 2, (x // 2) * 8 + (n % 4) * 2 + core)

    barrier = pltpu.get_barrier_semaphore()
    pl.semaphore_signal(barrier, inc=1, device_id=mate, device_id_type=MESH)
    for q in range(1, 4):
        pl.semaphore_signal(barrier, inc=1, device_id=z_id(q), device_id_type=MESH)
    for q in range(1, 16):
        pl.semaphore_signal(barrier, inc=1, device_id=plane_id(q), device_id_type=MESH)
    pl.semaphore_wait(barrier, 19)

    def block(start, count):
        return pl.ds(pl.multiple_of(start, 8), count)

    def send(src, dst, send_sem, recv_sem, device):
        return pltpu.make_async_remote_copy(
            src_ref=src, dst_ref=dst, send_sem=send_sem, recv_sem=recv_sem,
            device_id=device, device_id_type=MESH,
        )

    def exchange(copies):
        for copy in copies:
            copy.start()
        for copy in copies:
            copy.wait()

    exchange([send(part.at[block((1 - core) * 512, 512)], got0, s_send.at[0], s_recv.at[0], mate)])
    acc0[...] = part[block(core * 512, 512), :] + got0[...]
    exchange([
        send(acc0.at[block(z_peer(q) * 128, 128)], got1.at[q - 1], z_send.at[q - 1], z_recv.at[q - 1], z_id(q))
        for q in range(1, 4)
    ])
    acc1[...] = acc0[block(z * 128, 128), :] + got1[0] + got1[1] + got1[2]
    exchange([
        send(acc1.at[block(plane_peer(q) * 8, 8)], got2.at[q - 1], n_send.at[q - 1], n_recv.at[q - 1], plane_id(q))
        for q in range(1, 16)
    ])
    mine = acc1[block(plane * 8, 8), :]
    for q in range(15):
        mine = mine + got2[q]
    base0 = core * 512
    base1 = base0 + z * 128
    own = block(base1 + plane * 8, 8)
    full[own, :] = mine
    exchange([
        send(full.at[own], full.at[own], n_send.at[14 + q], n_recv.at[14 + q], plane_id(q))
        for q in range(1, 16)
    ])
    own = block(base1, 128)
    exchange([
        send(full.at[own], full.at[own], z_send.at[2 + q], z_recv.at[2 + q], z_id(q))
        for q in range(1, 4)
    ])
    own = block(base0, 512)
    exchange([send(full.at[own], full.at[own], s_send.at[1], s_recv.at[1], mate)])
    for p in range(2):
        for half in range(2):
            out[p, :, pl.ds(H * half, H)] = full[pl.ds((2 * p + half) * W, W), :]


def total(part):
    dma = pltpu.SemaphoreType.DMA
    return pl.pallas_call(
        total_kernel,
        out_shape=jax.ShapeDtypeStruct((2, W, W), F32),
        in_specs=[pl.BlockSpec(memory_space=pltpu.VMEM)],
        out_specs=pl.BlockSpec(memory_space=pltpu.VMEM),
        scratch_shapes=[
            VMEM((1024, H), F32),
            VMEM((512, H), F32),
            VMEM((512, H), F32),
            VMEM((3, 128, H), F32),
            VMEM((128, H), F32),
            VMEM((15, 8, H), F32),
            dma((2,)), dma((2,)), dma((6,)), dma((6,)), dma((30,)), dma((30,)),
        ],
        compiler_params=pltpu.CompilerParams(collective_id=0, has_side_effects=True),
        name="total",
    )(part)


def fold_kernel(tile, right, below_l, below_r, out):
    out[:, :, W:] = tile[:, :, W:]
    out[:, :, :W] = tile[:, :, :W] + right[...]

    @pl.when(pl.program_id(0) < 2)
    def _():
        out[:, :, :W] += below_l[...]
        out[:, :, W:] += below_r[...]


def fold(tile, right, below_l, below_r):
    rows = lambda i: (0, i, 0)
    upper = lambda i: (0, jnp.minimum(i, 1), 0)
    return pl.pallas_call(
        fold_kernel,
        grid=(4,),
        out_shape=jax.ShapeDtypeStruct((2, 512, 512), F32),
        in_specs=[
            pl.BlockSpec((2, 128, 512), rows),
            pl.BlockSpec((2, 128, 256), rows),
            pl.BlockSpec((2, 128, 256), upper),
            pl.BlockSpec((2, 128, 256), upper),
        ],
        out_specs=pl.BlockSpec((2, 128, 512), rows),
        name="fold",
    )(tile, right, below_l, below_r)


def from_behind(value, axis, steps):
    count = lax.axis_size(axis)
    initial, last = (max(0, -steps), min(count, count - steps))
    return lax.ppermute(value, axis, [(source, source + steps) for source in range(initial, last)])


def on_device(object_tile, probe, amplitudes, positions, counts):
    right = from_behind(object_tile[:, :, :W], "col", -1)
    below_l = from_behind(object_tile[:, :W, :W], "row", -1)
    below_r = from_behind(object_tile[:, :W, W:], "row", -1)
    corner = from_behind(below_l, "col", -1)
    amps = reorder(amplitudes[0, 0])
    count = lax.dynamic_slice(counts[0], (lax.axis_index("col"),), (1,))
    g_tile, g_right, g_below_l, g_below_r, g_corner, part = run_slots(
        positions[0, 0], count, object_tile, right, below_l, below_r, corner, amps, probe
    )
    to_corner = from_behind(g_corner, "col", 1)
    to_below_r = from_behind(g_below_r, "row", 1)
    to_right = from_behind(g_right, "col", 1)
    to_below_l = from_behind(g_below_l + to_corner, "row", 1)
    probe_grad = total(part)
    return (fold(g_tile, to_right, to_below_l, to_below_r), probe_grad)


def solution(mesh):
    in_specs = (
        P(None, "row", "col"),
        P(),
        P("row", "col", None, None, None),
        P("row", "col", None, None),
        P("row", None),
    )
    out_specs = (P(None, "row", "col"), P())
    return jax.shard_map(
        on_device, mesh=mesh, in_specs=in_specs, out_specs=out_specs, check_vma=False
    )
```

time: 708 us -> 159 us (0.22); the launches traced: 698 us -> 158 us
  local copies, waits for them, and re-layouts: 198 us -> 5.64 us
  waiting for transfers between devices: 200 us -> 9.04 us
  matrix products: 152 us -> 0 us
  Pallas kernels: 0 us -> 108 us
  loops' own time: 64.3 us -> 0 us
  other arithmetic: 41.6 us -> 0.86 us
  between operations: 14.6 us -> 0.84 us
    dot_general x16 -> x0, matrix products: 152 us -> none  [the longest x2 29.8 us: both_sides(): jnp.einsum('sjk,kl->sjl', left_re, table_re, precision=highest)]
    psum x1 -> x0, waiting for transfers between devices: 135 us -> none  [on_device(): probe_grad = lax.psum(probe_part, ('row', 'col'))]
    pallas_call x0 -> x4, Pallas kernels: none -> 108 us  [the longest x1 63.4 us: total(): pl.pallas_call(total_kernel, out_shape=jax.ShapeDtypeStruct((2, W, W), F3...]
    dynamic_update_slice x16 -> x0, local copies, waits for them, and re-layouts: 106 us -> none  [add_window(): lax.dynamic_update_slice(grad_ext, current + obj_terms[index], (zero, off...]
    another operation x2 -> x0, loops' own time: 64.3 us -> none  [the longest x1 64.3 us: on_device(): grad_ext = lax.fori_loop(0, capacity, add_window, jnp.zeros_like(extended))]
    gather x48 -> x0, local copies, waits for them, and re-layouts: 63.4 us -> none
    ppermute x4 -> x8, waiting for transfers between devices: 64.6 us -> 9.04 us  [from_behind(): lax.ppermute(value, axis, [(source, source + steps) for source in range(i...]
    add x16 -> x1, other arithmetic: 24.5 us -> 0.86 us  [on_device(): to_below_l = from_behind(g_below_l + to_corner, 'row', 1)]
  transfers between devices with their start and end apart: 5 -> 8, of which waited for: 5 -> 1; matrix products, arithmetic and copies ran while one was open for 2% -> 1% of each run, Pallas kernels for 0% -> 48%
where the time goes in v1:
time: 159 us; the launch traced here: 158 us
  Pallas kernels  108 us (68%)
  starting transfers between devices  33.3 us (21%)
  waiting for transfers between devices  9.04 us (6%)
  local copies, waits for them, and re-layouts  5.64 us (4%)
    pallas_call x1, Pallas kernels, total(): pl.pallas_call(total_kernel, out_shape=jax.ShapeDtypeStruct((2, W, W), F3...  63.4 us
    ppermute x8, starting transfers between devices, from_behind(): lax.ppermute(value, axis, [(source, source + steps) for source in range(i...  33.3 us
    pallas_call x1, Pallas kernels, run_slots(): pl.pallas_call(slots_kernel, out_shape=(block(2, 512, 512), block(2, 512,...  27.6 us
    pallas_call x1, Pallas kernels, reorder(): pl.pallas_call(reorder_kernel, grid=(amps.shape[0],), out_shape=jax.Shape...  13.3 us
    ppermute x8, waiting for transfers between devices, from_behind(): lax.ppermute(value, axis, [(source, source + steps) for source in range(i...  9.04 us
    pallas_call x1, Pallas kernels, fold(): pl.pallas_call(fold_kernel, grid=(4,), out_shape=jax.ShapeDtypeStruct((2,...  4.22 us
  transfers between devices with their start and end apart: 8, of which 1 were waited for; matrix products, arithmetic and copies ran while one was open for 1% of the time, Pallas kernels for 48%

profile of v1, /device:TPU:1, one launch (start us, length us, event | category | flops | bytes accessed | tf_op | source)
XLA Modules:
  0.0 158.2 jit_solution(6162179009926597937)
XLA Ops:
  0.6 0.0 copy-start
  0.6 0.0 copy-start.3
  0.7 0.0 copy-start.8
  0.7 2.2 %fusion = (f32[2,256,256]{2,1,0:T(8,128)}, f32[2,256,256]{2,1,0:T(8,128)S(1)}) fusion(f32[2,512,512]{2,1,0:T(8,128)} %tile.1), kind=kLoop, calls=%fused_computation.1 | loop fusion | bytes 2097152 | tf_op jit(solution)/shard_map/slice | solution.py:426
  2.9 1.3 collective-permute-start.1
  4.2 0.0 copy-done.3
  4.2 0.1 slice.9
  4.3 3.3 %collective-permute-start = (f32[2,512,256]{2,1,0:T(8,128)S(1)}, f32[2,512,256]{2,1,0:T(8,128)}, u32[]{:S(2)}, u32[]{:S(2)}) collective-permute-start(f32[2,512,256]{2,1,0:T(8,128)S(1)} %slice.9), channel_id=1, source_target_pairs={{1,0},{2,1},{3,2},{4,3},{5,4},{6,5},{7,6},{8,7},{9,8},{10,9},{11,1... | collective-permute-start | bytes 3145736 | tf_op jit(solution)/shard_map/ppermute | solution.py:420
  7.6 1.3 collective-permute-start.2
  8.9 9.0 %collective-permute-done.1.below_l = f32[2,256,256]{2,1,0:T(8,128)S(1)} collective-permute-done((f32[2,256,256]{2,1,0:T(8,128)S(1)}, f32[2,256,256]{2,1,0:T(8,128)S(1)}, u32[]{:S(2)}, u32[]{:S(2)}) %collective-permute-start.1) | collective-permute-done | bytes 524320 | tf_op jit(solution)/shard_map/ppermute | solution.py:420
  18.0 5.0 %collective-permute-start.3 = (f32[2,256,256]{2,1,0:T(8,128)S(1)}, f32[2,256,256]{2,1,0:T(8,128)S(1)}, u32[]{:S(2)}, u32[]{:S(2)}) collective-permute-start(f32[2,256,256]{2,1,0:T(8,128)S(1)} %collective-permute-done.1.below_l), channel_id=1, source_target_pairs={{1,0},{2,1},{3,2},{4,3},{5,4},{6,5},{7,6},{8,7},{9,8},{10,9},{11,1... | collective-permute-start | bytes 1572872 | tf_op jit(solution)/shard_map/ppermute | solution.py:420
  22.9 0.0 copy-done.8
  23.0 0.1 copy.10.pos
  23.0 0.0 copy-done
  23.0 0.6 constant_dynamic-slice_fusion
  23.6 0.0 copy-start.1
  23.6 13.3 %reorder.1.amps = f32[16,256,256]{2,1,0:T(8,128)} custom-call(f32[16,256,256]{2,1,0:T(8,128)} %bitcast.3, f32[16,256,256]{2,1,0:T(8,128)} %bitcast.4, f32[256,256]{1,0:T(8,128)} %constant.15.clone.select_t), custom_call_target="tpu_custom_call" | custom-call | tf_op jit(solution)/shard_map/reorder/pallas_call | solution.py:272
  36.9 0.0 collective-permute-done.2.below_r
  36.9 0.0 collective-permute-done.3.corner
  36.9 0.0 collective-permute-done.right
  36.9 0.0 copy-done.1
  36.9 27.6 %slots.1 = (f32[2,512,512]{2,1,0:T(8,128)}, f32[2,512,256]{2,1,0:T(8,128)S(1)}, f32[2,256,256]{2,1,0:T(8,128)S(1)}, f32[2,256,256]{2,1,0:T(8,128)}, f32[2,256,256]{2,1,0:T(8,128)S(1)}, /*index=5*/f32[1024,128]{1,0:T(8,128)S(1)}) custom-call(s32[16,2]{1,0:T(8,128)S(1)} %copy.10.pos, s32[1]{0:T(128)} %bitcast.1.cnt, f32[2,512,512]{2,1,0:T(8,128)} %tile.1, ...), custom_call_target="tpu_custom_call" | custom-call | tf_op jit(solution)/shard_map/slots/pallas_call | solution.py:228
  64.5 0.0 copy-start.2
  64.5 1.9 %collective-permute-start.5 = (f32[2,256,256]{2,1,0:T(8,128)S(1)}, f32[2,256,256]{2,1,0:T(8,128)S(1)}, u32[]{:S(2)}, u32[]{:S(2)}) collective-permute-start(f32[2,256,256]{2,1,0:T(8,128)S(1)} %get-tuple-element.11), channel_id=1, source_target_pairs={{0,1},{1,2},{2,3},{3,4},{4,5},{5,6},{6,7},{7,8},{8,9},{9,10},{10,1... | collective-permute-start | bytes 1572872 | tf_op jit(solution)/shard_map/ppermute | solution.py:420
  66.5 1.9 %collective-permute-start.4 = (f32[2,512,256]{2,1,0:T(8,128)S(1)}, f32[2,512,256]{2,1,0:T(8,128)S(1)}, u32[]{:S(2)}, u32[]{:S(2)}) collective-permute-start(f32[2,512,256]{2,1,0:T(8,128)S(1)} %get-tuple-element.9), channel_id=1, source_target_pairs={{0,1},{1,2},{2,3},{3,4},{4,5},{5,6},{6,7},{7,8},{8,9},{9,10},{10,1... | collective-permute-start | bytes 3145736 | tf_op jit(solution)/shard_map/ppermute | solution.py:420
  68.4 16.5 %collective-permute-start.7 = (f32[2,256,256]{2,1,0:T(8,128)}, f32[2,256,256]{2,1,0:T(8,128)S(1)}, u32[]{:S(2)}, u32[]{:S(2)}) collective-permute-start(f32[2,256,256]{2,1,0:T(8,128)} %get-tuple-element.12), channel_id=1, source_target_pairs={{0,16},{16,32},{32,48},{48,64},{64,80},{80,96},{96,112},{1,17},{17... | collective-permute-start | bytes 1572872 | tf_op jit(solution)/shard_map/ppermute | solution.py:420
  84.9 0.0 collective-permute-done.5
  84.9 0.9 add.7
  85.8 0.0 copy-done.2
  85.8 2.1 %collective-permute-start.6 = (f32[2,256,256]{2,1,0:T(8,128)}, f32[2,256,256]{2,1,0:T(8,128)S(1)}, u32[]{:S(2)}, u32[]{:S(2)}) collective-permute-start(f32[2,256,256]{2,1,0:T(8,128)} %add.7), channel_id=1, source_target_pairs={{0,16},{16,32},{32,48},{48,64},{64,80},{80,96},{96,112},{1,17},{17... | collective-permute-start | bytes 1572872 | tf_op jit(solution)/shard_map/ppermute | solution.py:420
  87.9 63.4 %total.1 = f32[2,256,256]{2,1,0:T(8,128)} custom-call(f32[1024,128]{1,0:T(8,128)} %copy-done.2), custom_call_target="tpu_custom_call" | custom-call | tf_op jit(solution)/shard_map/total/pallas_call | solution.py:370
  151.3 0.0 collective-permute-done.7.below_r
  151.3 0.0 copy-start.6
  151.3 0.0 collective-permute-done.6.below_l
  151.3 0.0 copy-start.7
  151.3 0.0 collective-permute-done.4.right
  151.4 0.8 copy-done.7
  152.2 0.0 copy-start.5
  152.2 0.1 copy-done.6
  152.3 0.9 copy-done.5
  153.2 0.0 copy-start.4
  153.2 4.2 %fold.1 = f32[2,512,512]{2,1,0:T(8,128)} custom-call(f32[2,512,512]{2,1,0:T(8,128)} %get-tuple-element.8.tile, f32[2,512,256]{2,1,0:T(8,128)} %copy-done.5, f32[2,256,256]{2,1,0:T(8,128)} %copy-done.7, f32[2,256,256]{2,1,0:T(8,128)} %copy-done.6), custom_call_target="tpu_custom_call" | custom-call | tf_op jit(solution)/shard_map/fold/pallas_call | solution.py:402
  157.4 0.0 copy-done.4
  157.4 0.8 copy.12
Async XLA Ops:
  0.6 22.4 %copy-start = (s32[1,16]{1,0:T(1,128)S(1)}, s32[1,16]{1,0:T(1,128)}, u32[]{:S(2)}) copy-start(s32[1,16]{1,0:T(1,128)} %param.12) | copy-start | bytes 196
  0.6 3.5 %copy-start.3 = (f32[2,512,512]{2,1,0:T(8,128)S(1)}, f32[2,512,512]{2,1,0:T(8,128)}, u32[]{:S(2)}) copy-start(f32[2,512,512]{2,1,0:T(8,128)} %tile.1) | copy-start | bytes 6291460
  0.7 22.3 %copy-start.8 = (s32[1,1,16,2]{2,3,1,0:T(2,128)S(1)}, s32[1,1,16,2]{2,3,1,0:T(2,128)}, u32[]{:S(2)}) copy-start(s32[1,1,16,2]{2,3,1,0:T(2,128)} %param.11) | copy-start | bytes 388
  2.9 15.1 %collective-permute-start.1 = (f32[2,256,256]{2,1,0:T(8,128)S(1)}, f32[2,256,256]{2,1,0:T(8,128)S(1)}, u32[]{:S(2)}, u32[]{:S(2)}) collective-permute-start(f32[2,256,256]{2,1,0:T(8,128)S(1)} %get-tuple-element.15), channel_id=1, source_target_pairs={{16,0},{32,16},{48,32},{64,48},{80,64},{96,80},{112,96},{17,1},{33... | collective-permute-start | bytes 1572872 | tf_op jit(solution)/shard_map/ppermute | solution.py:420
  4.3 32.6 %collective-permute-start = (f32[2,512,256]{2,1,0:T(8,128)S(1)}, f32[2,512,256]{2,1,0:T(8,128)}, u32[]{:S(2)}, u32[]{:S(2)}) collective-permute-start(f32[2,512,256]{2,1,0:T(8,128)S(1)} %slice.9), channel_id=1, source_target_pairs={{1,0},{2,1},{3,2},{4,3},{5,4},{6,5},{7,6},{8,7},{9,8},{10,9},{11,1... | collective-permute-start | bytes 3145736 | tf_op jit(solution)/shard_map/ppermute | solution.py:420
  7.6 29.3 %collective-permute-start.2 = (f32[2,256,256]{2,1,0:T(8,128)}, f32[2,256,256]{2,1,0:T(8,128)S(1)}, u32[]{:S(2)}, u32[]{:S(2)}) collective-permute-start(f32[2,256,256]{2,1,0:T(8,128)} %get-tuple-element.14), channel_id=1, source_target_pairs={{16,0},{32,16},{48,32},{64,48},{80,64},{96,80},{112,96},{17,1},{33... | collective-permute-start | bytes 1572872 | tf_op jit(solution)/shard_map/ppermute | solution.py:420
  18.0 18.9 %collective-permute-start.3 = (f32[2,256,256]{2,1,0:T(8,128)S(1)}, f32[2,256,256]{2,1,0:T(8,128)S(1)}, u32[]{:S(2)}, u32[]{:S(2)}) collective-permute-start(f32[2,256,256]{2,1,0:T(8,128)S(1)} %collective-permute-done.1.below_l), channel_id=1, source_target_pairs={{1,0},{2,1},{3,2},{4,3},{5,4},{6,5},{7,6},{8,7},{9,8},{10,9},{11,1... | collective-permute-start | bytes 1572872 | tf_op jit(solution)/shard_map/ppermute | solution.py:420
  23.6 13.3 %copy-start.1 = (f32[2,256,256]{2,1,0:T(8,128)S(1)}, f32[2,256,256]{2,1,0:T(8,128)}, u32[]{:S(2)}) copy-start(f32[2,256,256]{2,1,0:T(8,128)} %probe.1) | copy-start | bytes 1572868
  64.5 21.2 %copy-start.2 = (f32[1024,128]{1,0:T(8,128)}, f32[1024,128]{1,0:T(8,128)S(1)}, u32[]{:S(2)}) copy-start(f32[1024,128]{1,0:T(8,128)S(1)} %get-tuple-element.13.part) | copy-start | bytes 1572868
  64.5 20.4 %collective-permute-start.5 = (f32[2,256,256]{2,1,0:T(8,128)S(1)}, f32[2,256,256]{2,1,0:T(8,128)S(1)}, u32[]{:S(2)}, u32[]{:S(2)}) collective-permute-start(f32[2,256,256]{2,1,0:T(8,128)S(1)} %get-tuple-element.11), channel_id=1, source_target_pairs={{0,1},{1,2},{2,3},{3,4},{4,5},{5,6},{6,7},{7,8},{8,9},{9,10},{10,1... | collective-permute-start | bytes 1572872 | tf_op jit(solution)/shard_map/ppermute | solution.py:420
  66.5 84.9 %collective-permute-start.4 = (f32[2,512,256]{2,1,0:T(8,128)S(1)}, f32[2,512,256]{2,1,0:T(8,128)S(1)}, u32[]{:S(2)}, u32[]{:S(2)}) collective-permute-start(f32[2,512,256]{2,1,0:T(8,128)S(1)} %get-tuple-element.9), channel_id=1, source_target_pairs={{0,1},{1,2},{2,3},{3,4},{4,5},{5,6},{6,7},{7,8},{8,9},{9,10},{10,1... | collective-permute-start | bytes 3145736 | tf_op jit(solution)/shard_map/ppermute | solution.py:420
  68.4 82.9 %collective-permute-start.7 = (f32[2,256,256]{2,1,0:T(8,128)}, f32[2,256,256]{2,1,0:T(8,128)S(1)}, u32[]{:S(2)}, u32[]{:S(2)}) collective-permute-start(f32[2,256,256]{2,1,0:T(8,128)} %get-tuple-element.12), channel_id=1, source_target_pairs={{0,16},{16,32},{32,48},{48,64},{64,80},{80,96},{96,112},{1,17},{17... | collective-permute-start | bytes 1572872 | tf_op jit(solution)/shard_map/ppermute | solution.py:420
  85.8 65.6 %collective-permute-start.6 = (f32[2,256,256]{2,1,0:T(8,128)}, f32[2,256,256]{2,1,0:T(8,128)S(1)}, u32[]{:S(2)}, u32[]{:S(2)}) collective-permute-start(f32[2,256,256]{2,1,0:T(8,128)} %add.7), channel_id=1, source_target_pairs={{0,16},{16,32},{32,48},{48,64},{64,80},{80,96},{96,112},{1,17},{17... | collective-permute-start | bytes 1572872 | tf_op jit(solution)/shard_map/ppermute | solution.py:420
  151.3 1.0 copy-start.6
  151.3 0.9 copy-start.7
  152.2 1.0 copy-start.5
  153.2 4.2 %copy-start.4 = (f32[2,256,256]{2,1,0:T(8,128)S(1)}, f32[2,256,256]{2,1,0:T(8,128)}, u32[]{:S(2)}) copy-start(f32[2,256,256]{2,1,0:T(8,128)} %total.1) | copy-start | bytes 1572868

commit v2 on v1

--- a/solution.py
+++ b/solution.py
@@ -253,189 +253,366 @@
     )(own_pos, count, tile, right, below_l, below_r, corner, amps, probe, jnp.asarray(right_t), jnp.asarray(left_t))
 
 
-def reorder_kernel(amp_l, amp_r, select_t, amp_out):
-    half = jnp.concatenate(
-        [
-            jnp.concatenate([ref[0, pl.ds(start, H, stride=2), :] for ref in (amp_l, amp_r)], axis=1)
-            for start in range(2)
+MESH = pl.DeviceIdType.MESH
+N_ROW, N_COL = 8, 16
+SEAM = 7
+HEAD = 64
+AHEAD_Y, BACK_Y = 0, 3
+ANY = pl.ANY
+
+
+def place():
+    row, col = lax.axis_index("row"), lax.axis_index("col")
+    z, x_lo = row // 2, row % 2
+    x_hi, y, core = col // 8, (col // 2) % 4, col % 2
+    return row, col, x_hi * 2 + x_lo, y, z, core
+
+
+def at_chip(x, y, z, core):
+    return (z * 2 + x % 2, (x // 2) * 8 + y * 2 + core)
+
+
+def remote(src, dst, sems, n, device):
+    return pltpu.make_async_remote_copy(
+        src_ref=src, dst_ref=dst, send_sem=sems[0].at[n], recv_sem=sems[1].at[n],
+        device_id=device, device_id_type=MESH,
+    )
+
+
+def block(start, count):
+    return pl.ds(pl.multiple_of(start, 8), count)
+
+
+def greet(devices):
+    barrier = pltpu.get_barrier_semaphore()
+    for device in devices:
+        pl.semaphore_signal(barrier, inc=1, device_id=device, device_id_type=MESH)
+    return barrier
+
+
+def back_kernel(
+    g_tile, g_right, g_below_l, g_below_r, g_corner, part, out, out_p,
+    corner_in, right_in, below_l_in, below_r_in, seam_in, relay_in, below_sum,
+    full, got0, acc0, got1, acc1, got2,
+    h_send, h_recv, m_send, m_recv, p_send, p_recv, x_send, x_recv,
+):
+    row, col, x, y, z, core = place()
+    down, up = ((row + 1) % N_ROW, col), ((row + N_ROW - 1) % N_ROW, col)
+    right, left = (row, (col + 1) % N_COL), (row, (col + N_COL - 1) % N_COL)
+    mate = (row, col + 1 - 2 * core)
+    group = z * 4 + y
+
+    def group_peer(q):
+        return (group + q) % 16
+
+    def group_id(q):
+        n = group_peer(q)
+        return at_chip(x, n % 4, n // 4, core)
+
+    def x_id(q):
+        return at_chip((x + q) % 4, y, z, core)
+
+    at_seam, past_seam = col == SEAM, col == SEAM + 1
+    x_plus, x_minus = (x + 1) % 4, (x + 3) % 4
+    is_relay = (y == BACK_Y) & (core == x // 2)
+    has_down, has_up = row < N_ROW - 1, row > 0
+    sends_right = (col < N_COL - 1) & (col != SEAM)
+    gets_left = (col > 0) & (col != SEAM + 1)
+    relay_plus = at_chip(x_plus, BACK_Y, z, x_plus // 2)
+    relay_minus = at_chip(x_minus, BACK_Y, z, x_minus // 2)
+    serves_upper = (x == 1) | (x == 2)
+    relay_source = at_chip(jnp.where(serves_upper, x_minus, x_plus), 3, z, 1)
+    relay_dest = at_chip(jnp.where(serves_upper, x_plus, x_minus), 0, z, 0)
+    diagonal = ((row + 1) % N_ROW, SEAM + 1)
+    diagonal_from = ((row + N_ROW - 1) % N_ROW, SEAM)
+
+    barrier = greet([mate, down, up, left, right] + [group_id(q) for q in range(1, 16)] + [x_id(q) for q in range(1, 4)])
+
+    @pl.when(at_seam)
+    def _():
+        greet([relay_plus, relay_minus, diagonal])
+
+    @pl.when(past_seam)
+    def _():
+        greet([relay_plus, relay_minus, diagonal_from])
+
+    @pl.when(is_relay)
+    def _():
+        greet([relay_source, relay_dest])
+
+    extra = jnp.where(at_seam | past_seam, 3, 0) + jnp.where(is_relay, 2, 0)
+    pl.semaphore_wait(barrier, 23 + extra)
+
+    halo = (h_send, h_recv)
+    corner = remote(g_corner, corner_in, halo, 0, right)
+    below_r = remote(g_below_r, below_r_in, halo, 1, down)
+    cols = remote(g_right, right_in, halo, 2, right)
+    head, tail = pl.ds(0, HEAD), pl.ds(HEAD, W - HEAD)
+    below_l = remote(below_sum.at[:, head, :], below_l_in.at[:, head, :], halo, 3, down)
+    below_l2 = remote(below_sum.at[:, tail, :], below_l_in.at[:, tail, :], halo, 9, down)
+    seam_corner = remote(g_corner, seam_in, halo, 4, diagonal)
+    upper, lower = pl.ds(0, W), pl.ds(W, W)
+    to_plus = remote(g_right.at[:, upper, :], relay_in, halo, 5, relay_plus)
+    to_minus = remote(g_right.at[:, lower, :], relay_in, (h_send, h_recv), 6, relay_minus)
+    relay_upper = remote(relay_in, right_in.at[:, upper, :], halo, 7, relay_dest)
+    relay_lower = remote(relay_in, right_in.at[:, lower, :], halo, 8, relay_dest)
+
+    def when(cond, *actions):
+        @pl.when(cond)
+        def _():
+            for action in actions:
+                action()
+
+    when(at_seam, to_plus.start, to_minus.start)
+    when(at_seam & has_down, seam_corner.start)
+    when(sends_right, corner.start)
+    when(has_down, below_r.start)
+    swap = remote(part.at[block((1 - core) * 512, 512)], got0, (m_send, m_recv), 0, mate)
+    swap.start()
+    swap.wait()
+    acc0[...] = part[block(core * 512, 512), :] + got0[...]
+    spread = [
+        remote(acc0.at[block(group_peer(q) * 32, 32)], got1.at[q - 1], (p_send, p_recv), q - 1, group_id(q))
+        for q in range(1, 16)
+    ]
+    for copy in spread:
+        copy.start()
+    when(sends_right, corner.wait_send, cols.start)
+    when(is_relay & serves_upper, to_plus.wait_recv, relay_upper.start)
+    when(is_relay & jnp.logical_not(serves_upper), to_minus.wait_recv, relay_lower.start)
+    below_sum[...] = g_below_l[...]
+
+    @pl.when(gets_left)
+    def _():
+        corner.wait_recv()
+        below_sum[...] += corner_in[...]
+
+    for copy in spread:
+        copy.wait()
+    total = acc0[block(group * 32, 32), :]
+    for q in range(15):
+        total = total + got1[q]
+    acc1[...] = total
+    spread = [
+        remote(acc1.at[block((x + q) % 4 * 8, 8)], got2.at[q - 1], (x_send, x_recv), q - 1, x_id(q))
+        for q in range(1, 4)
+    ]
+    for copy in spread:
+        copy.start()
+    when(has_down, below_l.start)
+    for copy in spread:
+        copy.wait()
+    base1 = core * 512 + group * 32
+    own = block(base1 + x * 8, 8)
+    full[own, :] = acc1[block(x * 8, 8), :] + got2[0] + got2[1] + got2[2]
+
+    def gather(copies):
+        for copy in copies:
+            copy.start()
+        for copy in copies:
+            copy.wait()
+
+    spread = [remote(full.at[own], full.at[own], (x_send, x_recv), 2 + q, x_id(q)) for q in range(1, 4)]
+    for copy in spread:
+        copy.start()
+    when(has_down, below_l2.start)
+    for copy in spread:
+        copy.wait()
+    own1 = block(base1, 32)
+    gather([remote(full.at[own1], full.at[own1], (p_send, p_recv), 14 + q, group_id(q)) for q in range(1, 16)])
+    own0 = block(core * 512, 512)
+    gather([remote(full.at[own0], full.at[own0], (m_send, m_recv), 1, mate)])
+    for p in range(2):
+        for half in range(2):
+            out_p[p, :, pl.ds(H * half, H)] = full[pl.ds((2 * p + half) * W, W), :]
+
+    out[...] = g_tile[...]
+
+    @pl.when(has_up)
+    def _():
+        below_r.wait_recv()
+        out[:, :W, W:] += below_r_in[...]
+        below_l.wait_recv()
+        below_l2.wait_recv()
+        out[:, :W, :W] += below_l_in[...]
+
+    @pl.when(gets_left)
+    def _():
+        cols.wait_recv()
+        out[:, :, :W] += right_in[...]
+
+    @pl.when(past_seam)
+    def _():
+        relay_upper.wait_recv()
+        relay_lower.wait_recv()
+        out[:, :, :W] += right_in[...]
+
+    @pl.when(past_seam & has_up)
+    def _():
+        seam_corner.wait_recv()
+        out[:, :W, :W] += seam_in[...]
+
+    when(sends_right, cols.wait_send)
+    when(has_down, below_r.wait_send, below_l.wait_send, below_l2.wait_send)
+    when(at_seam, to_plus.wait_send, to_minus.wait_send)
+    when(at_seam & has_down, seam_corner.wait_send)
+    when(is_relay & serves_upper, relay_upper.wait_send)
+    when(is_relay & jnp.logical_not(serves_upper), relay_lower.wait_send)
+
+
+def back(g_tile, g_right, g_below_l, g_below_r, g_corner, part):
+    dma = pltpu.SemaphoreType.DMA
+    vmem = pl.BlockSpec(memory_space=pltpu.VMEM)
+    square = VMEM((2, W, W), F32)
+    return pl.pallas_call(
+        back_kernel,
+        out_shape=(jax.ShapeDtypeStruct((2, 512, 512), F32), jax.ShapeDtypeStruct((2, W, W), F32)),
+        in_specs=[vmem] * 6,
+        out_specs=(vmem, vmem),
+        scratch_shapes=[
+            square, VMEM((2, 512, W), F32), square, square, square, square, square,
+            VMEM((1024, H), F32), VMEM((512, H), F32), VMEM((512, H), F32),
+            VMEM((15, 32, H), F32), VMEM((32, H), F32), VMEM((3, 8, H), F32),
+            dma((10,)), dma((10,)), dma((2,)), dma((2,)), dma((30,)), dma((30,)), dma((6,)), dma((6,)),
         ],
-        axis=0,
-    )
-    amp_out[0] = jnp.dot(half, select_t[...], precision=lax.Precision.HIGHEST, preferred_element_type=F32)
-
-
-def reorder(amps):
+        compiler_params=pltpu.CompilerParams(
+            collective_id=1, has_side_effects=True, vmem_limit_bytes=40 * 1024 * 1024
+        ),
+        name="back",
+    )(g_tile, g_right, g_below_l, g_below_r, g_corner, part)
+
+
+def ahead_kernel(
+    tile, amps, select_t, right, below_l, below_r, corner, amps_out,
+    relay_in, amp_buf, h_send, h_recv, a_sem,
+):
+    row, col, x, y, z, core = place()
+    down, up = ((row + 1) % N_ROW, col), ((row + N_ROW - 1) % N_ROW, col)
+    to_right, to_left = (row, (col + 1) % N_COL), (row, (col + N_COL - 1) % N_COL)
+    at_seam, past_seam = col == SEAM, col == SEAM + 1
+    is_relay = (y == AHEAD_Y) & (core == x // 2)
+    has_down, has_up = row < N_ROW - 1, row > 0
+    sends_left = (col > 0) & (col != SEAM + 1)
+    gets_right = (col < N_COL - 1) & (col != SEAM)
+    x_plus, x_minus = (x + 1) % 4, (x + 3) % 4
+    relay_plus, relay_minus = at_chip(x_plus, AHEAD_Y, z, x_plus // 2), at_chip(x_minus, AHEAD_Y, z, x_minus // 2)
+    serves_upper = (x == 3) | (x == 0)
+    relay_source = at_chip(jnp.where(serves_upper, x_minus, x_plus), 0, z, 0)
+    relay_dest = at_chip(jnp.where(serves_upper, x_plus, x_minus), 3, z, 1)
+
+    def when(cond, *actions):
+        @pl.when(cond)
+        def _():
+            for action in actions:
+                action()
+
+    halves = [
+        pltpu.make_async_copy(amps.at[:, :, pl.ds(H * n, H)], amp_buf.at[:, n], a_sem.at[n])
+        for n in range(2)
+    ]
+    for copy in halves:
+        copy.start()
+    barrier = greet([down, up, to_left, to_right])
+
+    @pl.when(past_seam)
+    def _():
+        greet([relay_plus, relay_minus, ((row + N_ROW - 1) % N_ROW, SEAM)])
+
+    @pl.when(at_seam)
+    def _():
+        greet([relay_plus, relay_minus, ((row + 1) % N_ROW, SEAM + 1)])
+
+    @pl.when(is_relay)
+    def _():
+        greet([relay_source, relay_dest])
+
+    extra = jnp.where(at_seam | past_seam, 3, 0) + jnp.where(is_relay, 2, 0)
+    pl.semaphore_wait(barrier, 4 + extra)
+
+    halo = (h_send, h_recv)
+    upper, lower, every = pl.ds(0, W), pl.ds(W, W), pl.ds(0, 512)
+    first, last = pl.ds(0, W), pl.ds(W, W)
+    cols = remote(tile.at[:, every, first], right, halo, 0, to_left)
+    rows_l = remote(tile.at[:, upper, first], below_l, halo, 1, up)
+    rows_r = remote(tile.at[:, upper, last], below_r, halo, 2, up)
+    on_left = remote(below_l, corner, halo, 3, to_left)
+    seam_corner = remote(tile.at[:, upper, first], corner, halo, 4, ((row + N_ROW - 1) % N_ROW, SEAM))
+    to_plus = remote(tile.at[:, upper, first], relay_in, halo, 5, relay_plus)
+    to_minus = remote(tile.at[:, lower, first], relay_in, halo, 6, relay_minus)
+    relay_upper = remote(relay_in, right.at[:, upper, :], halo, 7, relay_dest)
+    relay_lower = remote(relay_in, right.at[:, lower, :], halo, 8, relay_dest)
+
+    when(past_seam, to_plus.start, to_minus.start)
+    when(past_seam & has_up, seam_corner.start)
+    when(has_up, rows_l.start)
+    when(sends_left, cols.start)
+    when(has_up & jnp.logical_not(is_relay), rows_r.start)
+    for copy in halves:
+        copy.wait()
+
+    def reorder_slot(k, _):
+        half = jnp.concatenate(
+            [
+                jnp.concatenate([amp_buf[k, n, pl.ds(start, H, stride=2), :] for n in range(2)], axis=1)
+                for start in range(2)
+            ],
+            axis=0,
+        )
+        high, mid = high_low(half)
+        low = (half - high.astype(F32) - mid.astype(F32)).astype(BF16)
+        amps_out[k] = dot(jnp.concatenate([high, mid, low], axis=1), select_t[...])
+        return 0
+
+    lax.fori_loop(0, amps.shape[0], reorder_slot, 0)
+    when(is_relay & serves_upper, to_plus.wait_recv, relay_upper.start)
+    when(is_relay & jnp.logical_not(serves_upper), to_minus.wait_recv, relay_lower.start)
+    when(is_relay & has_up, rows_r.start)
+    when(has_down, rows_l.wait_recv)
+    when(has_down & sends_left, on_left.start)
+    when(has_down, rows_r.wait_recv)
+    when(gets_right, cols.wait_recv)
+    when(at_seam, relay_upper.wait_recv, relay_lower.wait_recv)
+    when(gets_right & has_down, on_left.wait_recv)
+    when(at_seam & has_down, seam_corner.wait_recv)
+    when(sends_left, cols.wait_send)
+    when(has_up, rows_l.wait_send, rows_r.wait_send)
+    when(has_down & sends_left, on_left.wait_send)
+    when(past_seam, to_plus.wait_send, to_minus.wait_send)
+    when(past_seam & has_up, seam_corner.wait_send)
+    when(is_relay & serves_upper, relay_upper.wait_send)
+    when(is_relay & jnp.logical_not(serves_upper), relay_lower.wait_send)
+
+
+def ahead(tile, amps):
     n = np.arange(H)
     select = np.zeros((W, W), np.float32)
     select[2 * n, n] = 1.0
     select[2 * n + 1, H + n] = 1.0
+    select = jnp.asarray(np.concatenate([select] * 3, axis=0).astype(jnp.bfloat16))
+    dma = pltpu.SemaphoreType.DMA
+    vmem = pl.BlockSpec(memory_space=pltpu.VMEM)
+    any_spec = pl.BlockSpec(memory_space=pl.ANY)
+    square = jax.ShapeDtypeStruct((2, W, W), F32)
     return pl.pallas_call(
-        reorder_kernel,
-        grid=(amps.shape[0],),
-        out_shape=jax.ShapeDtypeStruct(amps.shape, F32),
-        in_specs=[
-            pl.BlockSpec((1, W, H), lambda k: (k, 0, 0)),
-            pl.BlockSpec((1, W, H), lambda k: (k, 0, 1)),
-            pl.BlockSpec((W, W), lambda k: (0, 0)),
-        ],
-        out_specs=pl.BlockSpec((1, W, W), lambda k: (k, 0, 0)),
-        name="reorder",
-    )(amps, amps, jnp.asarray(select))
-
-
-MESH = pl.DeviceIdType.MESH
-
-
-def total_kernel(part, out, full, got0, acc0, got1, acc1, got2, s_send, s_recv, z_send, z_recv, n_send, n_recv):
-    row, col = lax.axis_index("row"), lax.axis_index("col")
-    z, x_lo = row // 2, row % 2
-    x_hi, y, core = col // 8, (col // 2) % 4, col % 2
-    plane = (x_hi * 2 + x_lo) * 4 + y
-
-    mate = (row, col + 1 - 2 * core)
-
-    def z_peer(q):
-        return (z + q) % 4
-
-    def z_id(q):
-        return (z_peer(q) * 2 + x_lo, col)
-
-    def plane_peer(q):
-        return (plane + q) % 16
-
-    def plane_id(q):
-        n = plane_peer(q)
-        x = n // 4
-        return (z * 2 + x % 2, (x // 2) * 8 + (n % 4) * 2 + core)
-
-    barrier = pltpu.get_barrier_semaphore()
-    pl.semaphore_signal(barrier, inc=1, device_id=mate, device_id_type=MESH)
-    for q in range(1, 4):
-        pl.semaphore_signal(barrier, inc=1, device_id=z_id(q), device_id_type=MESH)
-    for q in range(1, 16):
-        pl.semaphore_signal(barrier, inc=1, device_id=plane_id(q), device_id_type=MESH)
-    pl.semaphore_wait(barrier, 19)
-
-    def block(start, count):
-        return pl.ds(pl.multiple_of(start, 8), count)
-
-    def send(src, dst, send_sem, recv_sem, device):
-        return pltpu.make_async_remote_copy(
-            src_ref=src, dst_ref=dst, send_sem=send_sem, recv_sem=recv_sem,
-            device_id=device, device_id_type=MESH,
-        )
-
-    def exchange(copies):
-        for copy in copies:
-            copy.start()
-        for copy in copies:
-            copy.wait()
-
-    exchange([send(part.at[block((1 - core) * 512, 512)], got0, s_send.at[0], s_recv.at[0], mate)])
-    acc0[...] = part[block(core * 512, 512), :] + got0[...]
-    exchange([
-        send(acc0.at[block(z_peer(q) * 128, 128)], got1.at[q - 1], z_send.at[q - 1], z_recv.at[q - 1], z_id(q))
-        for q in range(1, 4)
-    ])
-    acc1[...] = acc0[block(z * 128, 128), :] + got1[0] + got1[1] + got1[2]
-    exchange([
-        send(acc1.at[block(plane_peer(q) * 8, 8)], got2.at[q - 1], n_send.at[q - 1], n_recv.at[q - 1], plane_id(q))
-        for q in range(1, 16)
-    ])
-    mine = acc1[block(plane * 8, 8), :]
-    for q in range(15):
-        mine = mine + got2[q]
-    base0 = core * 512
-    base1 = base0 + z * 128
-    own = block(base1 + plane * 8, 8)
-    full[own, :] = mine
-    exchange([
-        send(full.at[own], full.at[own], n_send.at[14 + q], n_recv.at[14 + q], plane_id(q))
-        for q in range(1, 16)
-    ])
-    own = block(base1, 128)
-    exchange([
-        send(full.at[own], full.at[own], z_send.at[2 + q], z_recv.at[2 + q], z_id(q))
-        for q in range(1, 4)
-    ])
-    own = block(base0, 512)
-    exchange([send(full.at[own], full.at[own], s_send.at[1], s_recv.at[1], mate)])
-    for p in range(2):
-        for half in range(2):
-            out[p, :, pl.ds(H * half, H)] = full[pl.ds((2 * p + half) * W, W), :]
-
-
-def total(part):
-    dma = pltpu.SemaphoreType.DMA
-    return pl.pallas_call(
-        total_kernel,
-        out_shape=jax.ShapeDtypeStruct((2, W, W), F32),
-        in_specs=[pl.BlockSpec(memory_space=pltpu.VMEM)],
-        out_specs=pl.BlockSpec(memory_space=pltpu.VMEM),
-        scratch_shapes=[
-            VMEM((1024, H), F32),
-            VMEM((512, H), F32),
-            VMEM((512, H), F32),
-            VMEM((3, 128, H), F32),
-            VMEM((128, H), F32),
-            VMEM((15, 8, H), F32),
-            dma((2,)), dma((2,)), dma((6,)), dma((6,)), dma((30,)), dma((30,)),
-        ],
-        compiler_params=pltpu.CompilerParams(collective_id=0, has_side_effects=True),
-        name="total",
-    )(part)
-
-
-def fold_kernel(tile, right, below_l, below_r, out):
-    out[:, :, W:] = tile[:, :, W:]
-    out[:, :, :W] = tile[:, :, :W] + right[...]
-
-    @pl.when(pl.program_id(0) < 2)
-    def _():
-        out[:, :, :W] += below_l[...]
-        out[:, :, W:] += below_r[...]
-
-
-def fold(tile, right, below_l, below_r):
-    rows = lambda i: (0, i, 0)
-    upper = lambda i: (0, jnp.minimum(i, 1), 0)
-    return pl.pallas_call(
-        fold_kernel,
-        grid=(4,),
-        out_shape=jax.ShapeDtypeStruct((2, 512, 512), F32),
-        in_specs=[
-            pl.BlockSpec((2, 128, 512), rows),
-            pl.BlockSpec((2, 128, 256), rows),
-            pl.BlockSpec((2, 128, 256), upper),
-            pl.BlockSpec((2, 128, 256), upper),
-        ],
-        out_specs=pl.BlockSpec((2, 128, 512), rows),
-        name="fold",
-    )(tile, right, below_l, below_r)
-
-
-def from_behind(value, axis, steps):
-    count = lax.axis_size(axis)
-    initial, last = (max(0, -steps), min(count, count - steps))
-    return lax.ppermute(value, axis, [(source, source + steps) for source in range(initial, last)])
+        ahead_kernel,
+        out_shape=(jax.ShapeDtypeStruct((2, 512, W), F32), square, square, square, jax.ShapeDtypeStruct(amps.shape, F32)),
+        in_specs=[any_spec, any_spec, vmem],
+        out_specs=(any_spec, any_spec, any_spec, any_spec, vmem),
+        scratch_shapes=[VMEM((2, W, W), F32), VMEM((amps.shape[0], 2, W, H), F32), dma((9,)), dma((9,)), dma((2,))],
+        compiler_params=pltpu.CompilerParams(
+            collective_id=0, has_side_effects=True, vmem_limit_bytes=40 * 1024 * 1024
+        ),
+        name="ahead",
+    )(tile, amps, select)
 
 
 def on_device(object_tile, probe, amplitudes, positions, counts):
-    right = from_behind(object_tile[:, :, :W], "col", -1)
-    below_l = from_behind(object_tile[:, :W, :W], "row", -1)
-    below_r = from_behind(object_tile[:, :W, W:], "row", -1)
-    corner = from_behind(below_l, "col", -1)
-    amps = reorder(amplitudes[0, 0])
+    right, below_l, below_r, corner, amps = ahead(object_tile, amplitudes[0, 0])
     count = lax.dynamic_slice(counts[0], (lax.axis_index("col"),), (1,))
     g_tile, g_right, g_below_l, g_below_r, g_corner, part = run_slots(
         positions[0, 0], count, object_tile, right, below_l, below_r, corner, amps, probe
     )
-    to_corner = from_behind(g_corner, "col", 1)
-    to_below_r = from_behind(g_below_r, "row", 1)
-    to_right = from_behind(g_right, "col", 1)
-    to_below_l = from_behind(g_below_l + to_corner, "row", 1)
-    probe_grad = total(part)
-    return (fold(g_tile, to_right, to_below_l, to_below_r), probe_grad)
+    return back(g_tile, g_right, g_below_l, g_below_r, g_corner, part)
 
 
 def solution(mesh):

time: 159 us -> 136 us (0.86)
  starting transfers between devices: 33.3 us -> 0 us
  Pallas kernels: 108 us -> 121 us
  waiting for transfers between devices: 9.04 us -> 0 us
  local copies, waits for them, and re-layouts: 5.64 us -> 13.4 us
    ppermute x8 -> x0, starting transfers between devices: 33.3 us -> none  [from_behind(): lax.ppermute(value, axis, [(source, source + steps) for source in range(i...]
    pallas_call x3 -> x2, Pallas kernels: 80.9 us -> 91.6 us  [the longest x1 65.4 us: back(): pl.pallas_call(back_kernel, out_shape=(jax.ShapeDtypeStruct((2, 512, 512)...]
    unnamed x19 -> x18, local copies, waits for them, and re-layouts: 2.64 us -> 12 us
    ppermute x8 -> x0, waiting for transfers between devices: 9.04 us -> none  [from_behind(): lax.ppermute(value, axis, [(source, source + steps) for source in range(i...]
    slice x2 -> x0, local copies, waits for them, and re-layouts: 2.33 us -> none  [the longest x1 2.22 us: on_device(): below_r = from_behind(object_tile[:, :W, W:], 'row', -1)]
    pallas_call x1, Pallas kernels: 27.6 us -> 29.5 us  [run_slots(): pl.pallas_call(slots_kernel, out_shape=(block(2, 512, 512), block(2, 512,...]
  transfers between devices with their start and end apart: 8 -> 0, of which waited for: 1 -> 0; matrix products, arithmetic and copies ran while one was open for 1% -> 0% of each run, Pallas kernels for 48% -> 0%
where the time goes in v2:
time: 136 us; the launch traced here: 135 us
  Pallas kernels  121 us (89%)
  local copies, waits for them, and re-layouts  13.4 us (10%)
    pallas_call x1, Pallas kernels, back(): pl.pallas_call(back_kernel, out_shape=(jax.ShapeDtypeStruct((2, 512, 512)...  65.4 us
    pallas_call x1, Pallas kernels, run_slots(): pl.pallas_call(slots_kernel, out_shape=(block(2, 512, 512), block(2, 512,...  29.5 us
    pallas_call x1, Pallas kernels, ahead(): pl.pallas_call(ahead_kernel, out_shape=(jax.ShapeDtypeStruct((2, 512, W),...  26.2 us
    unnamed x18, local copies, waits for them, and re-layouts  12 us

profile of v2, /device:TPU:1, one launch (start us, length us, event | category | flops | bytes accessed | tf_op | source)
XLA Modules:
  0.0 135.2 jit_solution(12714137880332319076)
XLA Ops:
  0.6 0.0 copy-start
  0.6 0.6 copy-done
  1.3 0.6 constant_dynamic-slice_fusion
  1.9 0.8 copy.10.pos
  2.6 0.0 copy-start.1
  2.6 1.6 %copy-done.1 = f32[2,512,512]{2,1,0:T(8,128)S(1)} copy-done((f32[2,512,512]{2,1,0:T(8,128)S(1)}, f32[2,512,512]{2,1,0:T(8,128)}, u32[]{:S(2)}) %copy-start.1) | copy-done | bytes 2097176
  4.2 0.0 copy-start.2
  4.2 2.2 %copy-done.2 = f32[1,1,16,256,256]{4,3,2,1,0:T(8,128)S(1)} copy-done((f32[1,1,16,256,256]{4,3,2,1,0:T(8,128)S(1)}, f32[1,1,16,256,256]{4,3,2,1,0:T(8,128)}, u32[]{:S(2)}) %copy-start.2) | copy-done | bytes 4194328
  6.4 0.0 copy-start.7
  6.4 1.0 copy-done.7
  7.4 0.0 copy-start.6
  7.4 26.2 %ahead.1 = (f32[2,512,256]{2,1,0:T(8,128)S(1)}, f32[2,256,256]{2,1,0:T(8,128)S(1)}, f32[2,256,256]{2,1,0:T(8,128)S(1)}, f32[2,256,256]{2,1,0:T(8,128)S(1)}, f32[16,256,256]{2,1,0:T(8,128)S(1)}) custom-call(f32[2,512,512]{2,1,0:T(8,128)S(1)} %copy-done.1, f32[16,256,256]{2,1,0:T(8,128)S(1)} %bitcast.3, bf16[768,256]{1,0:T(8,128)(2,1)S(1)} %copy-done.7), custom_call_target="tpu_custom_call" | custom-call | tf_op jit(solution)/shard_map/ahead/pallas_call | solution.py:596
  33.6 0.0 copy-start.3
  33.6 1.9 %copy-done.3 = f32[16,256,256]{2,1,0:T(8,128)} copy-done((f32[16,256,256]{2,1,0:T(8,128)}, f32[16,256,256]{2,1,0:T(8,128)S(1)}, u32[]{:S(2)}) %copy-start.3) | copy-done | bytes 4194328
  35.6 0.0 copy-start.5
  35.6 1.0 copy-done.5
  36.5 0.0 copy-done.6
  36.5 29.5 %slots.1 = (f32[2,512,512]{2,1,0:T(8,128)}, f32[2,512,256]{2,1,0:T(8,128)S(1)}, f32[2,256,256]{2,1,0:T(8,128)S(1)}, f32[2,256,256]{2,1,0:T(8,128)S(1)}, f32[2,25...) custom-call(s32[16,2]{1,0:T(8,128)S(1)} %copy.10.pos, s32[1]{0:T(128)} %bitcast.1.cnt, f32[2,512,512]{2,1,0:T(8,128)} %tile.3, ...), custom_call_target="tpu_custom_call" | custom-call | tf_op jit(solution)/shard_map/slots/pallas_call | solution.py:228
  66.1 0.0 copy-start.4
  66.1 1.6 %copy-done.4 = f32[2,512,512]{2,1,0:T(8,128)S(1)} copy-done((f32[2,512,512]{2,1,0:T(8,128)S(1)}, f32[2,512,512]{2,1,0:T(8,128)}, u32[]{:S(2)}) %copy-start.4) | copy-done | bytes 2097176
  67.7 65.4 %back.1 = (f32[2,512,512]{2,1,0:T(8,128)S(1)}, f32[2,256,256]{2,1,0:T(8,128)S(1)}) custom-call(f32[2,512,512]{2,1,0:T(8,128)S(1)} %copy-done.4, f32[2,512,256]{2,1,0:T(8,128)S(1)} %get-tuple-element.19.g_right, f32[2,256,256]{2,1,0:T(8,128)S(1)} %get-tuple-element.20.g_below_l, f32[2,256,256]{2,1,0:T(8,128)S(1)} %get-tuple-element.21.g_below_r, ...), custom_call_target="tpu_custom_call" | custom-call | tf_op jit(solution)/shard_map/back/pallas_call | solution.py:467
  133.1 1.3 copy.13
  134.4 0.8 copy.14
Async XLA Ops:
  0.6 0.7 copy-start
  2.6 1.6 %copy-start.1 = (f32[2,512,512]{2,1,0:T(8,128)S(1)}, f32[2,512,512]{2,1,0:T(8,128)}, u32[]{:S(2)}) copy-start(f32[2,512,512]{2,1,0:T(8,128)} %tile.3) | copy-start | bytes 6291460
  4.2 2.2 %copy-start.2 = (f32[1,1,16,256,256]{4,3,2,1,0:T(8,128)S(1)}, f32[1,1,16,256,256]{4,3,2,1,0:T(8,128)}, u32[]{:S(2)}) copy-start(f32[1,1,16,256,256]{4,3,2,1,0:T(8,128)} %param.10) | copy-start | bytes 12582916
  6.4 1.0 copy-start.7
  7.4 29.1 %copy-start.6 = (f32[2,256,256]{2,1,0:T(8,128)S(1)}, f32[2,256,256]{2,1,0:T(8,128)}, u32[]{:S(2)}) copy-start(f32[2,256,256]{2,1,0:T(8,128)} %probe.1) | copy-start | bytes 1572868
  33.6 1.9 %copy-start.3 = (f32[16,256,256]{2,1,0:T(8,128)}, f32[16,256,256]{2,1,0:T(8,128)S(1)}, u32[]{:S(2)}) copy-start(f32[16,256,256]{2,1,0:T(8,128)S(1)} %get-tuple-element.17.amps) | copy-start | bytes 12582916
  35.6 1.0 copy-start.5
  66.1 1.6 %copy-start.4 = (f32[2,512,512]{2,1,0:T(8,128)S(1)}, f32[2,512,512]{2,1,0:T(8,128)}, u32[]{:S(2)}) copy-start(f32[2,512,512]{2,1,0:T(8,128)} %get-tuple-element.18.g_tile) | copy-start | bytes 6291460

commit v3 on v2

v3 whole, which is shorter than its diff:
```python
import math

import jax
import jax.numpy as jnp
import numpy as np
from jax import lax
from jax.experimental import pallas as pl
from jax.experimental.pallas import tpu as pltpu
from jax.sharding import PartitionSpec as P

smooth_term = 0.01
F32 = jnp.float32
BF16 = jnp.bfloat16
W = 256
H = 128
T = 512
CH = 32
TILES = 6
VMEM = pltpu.VMEM
MESH = pl.DeviceIdType.MESH
N_ROW, N_COL = 8, 16
SEAM = 7
AHEAD_Y, BACK_Y = 0, 3
EXT = (2, TILES, T + W, H)
MIB = 1024 * 1024


def tables():
    n = np.arange(H)
    even = np.exp(-2j * np.pi * np.outer(n, n) / H) / math.sqrt(W)
    odd = np.exp(-2j * np.pi * n / W)[:, None] * even

    def real_form(z):
        return np.block([[z.real, z.imag], [-z.imag, z.real]])

    pair = [real_form(even), real_form(odd)]
    return np.stack(pair + [table.T for table in pair]).astype(np.float32)


def high_low(value):
    high = value.astype(BF16)
    return high, (value - high.astype(F32)).astype(BF16)


def put(ref, rows, cols, value):
    ref[0, rows, cols], ref[1, rows, cols] = high_low(value)


def dot(a, b):
    return jnp.dot(a, b, preferred_element_type=F32)


def by_right(x, t, n):
    return dot(x[0], t[n, 0]) + dot(x[1], t[n, 0]) + dot(x[0], t[n, 1])


def by_left(x, t, n):
    return dot(t[n, 0], x[0]) + dot(t[n, 0], x[1]) + dot(t[n, 1], x[0])


def slot_steps(r, c, live, ext, gext, probe, amp, t, win, xe, xo, ye, yo, pgrad):
    j0 = lax.shift_right_logical(c, 7)
    s = lax.bitwise_and(c, 127)
    back_shift = lax.bitwise_and(128 - s, 127)
    lane = lax.broadcasted_iota(jnp.int32, (CH, H), 1)
    first = lane < 128 - s
    left, right, both = pl.ds(0, H), pl.ds(H, H), pl.ds(0, W)
    for i in range(W // CH):
        rows = pl.ds(i * CH, CH)
        parts = []
        for p in range(2):
            q = [
                pltpu.roll(ext[p, j0 + n, pl.ds(r + i * CH, CH), :], back_shift, 1)
                for n in range(3)
            ]
            a = jnp.where(first, q[0], q[1])
            b = jnp.where(first, q[1], q[2])
            win[p, rows, left] = a
            win[p, rows, right] = b
            parts.append((a, b))
        (are, bre), (aim, bim) = parts
        pra, prb = probe[0, rows, left], probe[0, rows, right]
        pia, pib = probe[1, rows, left], probe[1, rows, right]
        ea_re = pra * are - pia * aim
        ea_im = pra * aim + pia * are
        eb_re = prb * bre - pib * bim
        eb_im = prb * bim + pib * bre
        put(xe, rows, left, ea_re + eb_re)
        put(xe, rows, right, ea_im + eb_im)
        put(xo, rows, left, ea_re - eb_re)
        put(xo, rows, right, ea_im - eb_im)
    yield
    ye[...] = by_right(xe, t, 0)
    yo[...] = by_right(xo, t, 1)
    yield
    for i in range(H // CH):
        top = pl.ds(i * CH, CH)
        bot = pl.ds(H + i * CH, CH)
        for cols, y in ((left, ye), (right, yo)):
            for part, lanes in ((0, left), (H, right)):
                a, b = y[top, lanes], y[bot, lanes]
                put(xe, pl.ds(part + i * CH, CH), cols, a + b)
                put(xo, pl.ds(part + i * CH, CH), cols, a - b)
    yield
    ye[...] = by_left(xe, t, 2)
    yo[...] = by_left(xo, t, 3)
    yield
    for i in range(H // CH):
        for at, y, x in ((0, ye, xe), (H, yo, xo)):
            re = y[pl.ds(i * CH, CH), :]
            im = y[pl.ds(H + i * CH, CH), :]
            a = amp[pl.ds(at + i * CH, CH), :]
            f = (2.0 - (2.0 * a) * lax.rsqrt(re * re + im * im + smooth_term)) * live
            put(x, pl.ds(i * CH, CH), both, f * re)
            put(x, pl.ds(H + i * CH, CH), both, f * im)
    yield
    ye[...] = by_left(xe, t, 0)
    yo[...] = by_left(xo, t, 1)
    yield
    for i in range(H // CH):
        for part, lanes in ((0, left), (H, right)):
            e = ye[pl.ds(part + i * CH, CH), :]
            o = yo[pl.ds(part + i * CH, CH), :]
            for at, value in ((0, e + o), (H, e - o)):
                rows = pl.ds(at + i * CH, CH)
                put(xe, rows, lanes, value[:, 0:H])
                put(xo, rows, lanes, value[:, H:W])
    yield
    ye[...] = by_right(xe, t, 2)
    yo[...] = by_right(xo, t, 3)
    yield
    later = lane >= s
    for i in range(W // CH):
        rows = pl.ds(i * CH, CH)
        e_re, e_im = ye[rows, left], ye[rows, right]
        o_re, o_im = yo[rows, left], yo[rows, right]
        terms = []
        for n, cols, b_re, b_im in ((0, left, e_re + o_re, e_im + o_im), (1, right, e_re - o_re, e_im - o_im)):
            pr, pi = probe[0, rows, cols], probe[1, rows, cols]
            wr, wi = win[0, rows, cols], win[1, rows, cols]
            pgrad[n, rows, :] += wr * b_re + wi * b_im
            pgrad[2 + n, rows, :] += wr * b_im - wi * b_re
            terms.append((pr * b_re + pi * b_im, pr * b_im - pi * b_re))
        for p in range(2):
            ra = pltpu.roll(terms[0][p], s, 1)
            rb = pltpu.roll(terms[1][p], s, 1)
            at = pl.ds(r + i * CH, CH)
            gext[p, j0, at, :] += jnp.where(later, ra, 0.0)
            gext[p, j0 + 1, at, :] += jnp.where(later, rb, ra)
            gext[p, j0 + 2, at, :] += jnp.where(later, 0.0, rb)
    yield


def interleave(streams, lag):
    waiting = [[stream, n * lag] for n, stream in enumerate(streams)]
    while waiting:
        for item in list(waiting):
            if item[1] > 0:
                item[1] -= 1
            elif next(item[0], waiting) is waiting:
                waiting.remove(item)


def slots_kernel(
    pos, counts, ext, amps, probe, table, gext, pgrad, amp_buf, t, win, xe, xo, ye, yo, amp_sem
):
    count = counts[0, lax.axis_index("col")]
    groups = lax.div(count + U - 1, U)

    def amp_copy(n, buf):
        return pltpu.make_async_copy(amps.at[pl.ds(U * n, U)], amp_buf.at[buf], amp_sem.at[buf])

    @pl.when(count > 0)
    def _():
        amp_copy(0, 0).start()

    gext[...] = jnp.zeros_like(gext)
    pgrad[...] = jnp.zeros_like(pgrad)
    for n in range(4):
        t[n, 0], t[n, 1] = high_low(table[n])

    def body(n, _):
        buf = lax.bitwise_and(n, 1)

        @pl.when(n + 1 < groups)
        def _():
            amp_copy(n + 1, 1 - buf).start()

        amp_copy(n, buf).wait()
        streams = []
        for u in range(U):
            k = U * n + u
            live = (k < count).astype(F32)
            streams.append(
                slot_steps(
                    pos[0, k], pos[1, k], live, ext, gext, probe, amp_buf.at[buf, u], t,
                    win.at[u], xe.at[u], xo.at[u], ye.at[u], yo.at[u], pgrad,
                )
            )
        interleave(streams, LAG)
        return 0

    lax.fori_loop(0, groups, body, 0)


LAG = 1
U = 4


def run_slots(own_pos, counts, ext, amps, probe):
    vmem = pl.BlockSpec(memory_space=pltpu.VMEM)
    smem = pl.BlockSpec(memory_space=pltpu.SMEM)
    return pl.pallas_call(
        slots_kernel,
        out_shape=(jax.ShapeDtypeStruct(EXT, F32), jax.ShapeDtypeStruct((4, W, H), F32)),
        in_specs=[smem, smem, vmem, pl.BlockSpec(memory_space=pl.ANY), vmem, vmem],
        out_specs=(vmem, vmem),
        scratch_shapes=[
            VMEM((2, U, W, W), F32),
            VMEM((4, 2, W, W), BF16),
            VMEM((U, 2, W, W), F32),
            VMEM((U, 2, W, W), BF16),
            VMEM((U, 2, W, W), BF16),
            VMEM((U, W, W), F32),
            VMEM((U, W, W), F32),
            pltpu.SemaphoreType.DMA((2,)),
        ],
        compiler_params=pltpu.CompilerParams(vmem_limit_bytes=40 * MIB),
        name="slots",
    )(own_pos, counts, ext, amps, probe, jnp.asarray(tables()))


def place():
    row, col = lax.axis_index("row"), lax.axis_index("col")
    z, x_lo = row // 2, row % 2
    x_hi, y, core = col // 8, (col // 2) % 4, col % 2
    return row, col, x_hi * 2 + x_lo, y, z, core


def at_chip(x, y, z, core):
    return (z * 2 + x % 2, (x // 2) * 8 + y * 2 + core)


def remote(src, dst, sems, n, device):
    return pltpu.make_async_remote_copy(
        src_ref=src, dst_ref=dst, send_sem=sems[0].at[n], recv_sem=sems[1].at[n],
        device_id=device, device_id_type=MESH,
    )


def block(start, count):
    return pl.ds(pl.multiple_of(start, 8), count)


def greet(devices):
    barrier = pltpu.get_barrier_semaphore()
    for device in devices:
        pl.semaphore_signal(barrier, inc=1, device_id=device, device_id_type=MESH)
    return barrier


def when(cond, *actions):
    @pl.when(cond)
    def _():
        for action in actions:
            action()


def area(ref, tile, row, rows):
    return ref.at[:, pl.ds(tile, 2), pl.ds(row, rows), :]


def back_kernel(
    gext, part, out, out_p, corner_in, right_in, below_l_in, below_r_in, seam_in, relay_in, below_sum,
    full, got0, acc0, got1, acc1, got2,
    h_send, h_recv, r_send, r_recv, m_send, m_recv, p_send, p_recv, x_send, x_recv,
):
    row, col, x, y, z, core = place()
    down, up = ((row + 1) % N_ROW, col), ((row + N_ROW - 1) % N_ROW, col)
    right, left = (row, (col + 1) % N_COL), (row, (col + N_COL - 1) % N_COL)
    mate = (row, col + 1 - 2 * core)
    pair, place_in_pair = (x + 1) // 2 % 2, x // 2
    near, far = place_in_pair * 4 + y, pair * 4 + z

    def near_peer(q):
        return (near + q) % 8

    def near_id(q):
        n = near_peer(q)
        return at_chip(pair + n // 4 * (3 - 2 * pair), n % 4, z, core)

    def far_peer(q):
        return (far + q) % 8

    def far_id(q):
        n = far_peer(q)
        return at_chip(n // 4 + place_in_pair * (3 - 2 * (n // 4)), y, n % 4, core)

    at_seam, past_seam = col == SEAM, col == SEAM + 1
    x_plus, x_minus = (x + 1) % 4, (x + 3) % 4
    is_relay = (y == BACK_Y) & (core == x // 2)
    has_down, has_up = row < N_ROW - 1, row > 0
    sends_right = (col < N_COL - 1) & (col != SEAM)
    gets_left = (col > 0) & (col != SEAM + 1)
    relay_plus = at_chip(x_plus, BACK_Y, z, x_plus // 2)
    relay_minus = at_chip(x_minus, BACK_Y, z, x_minus // 2)
    serves_upper = (x == 1) | (x == 2)
    relay_source = at_chip(jnp.where(serves_upper, x_minus, x_plus), 3, z, 1)
    relay_dest = at_chip(jnp.where(serves_upper, x_plus, x_minus), 0, z, 0)
    diagonal = ((row + 1) % N_ROW, SEAM + 1)
    diagonal_from = ((row + N_ROW - 1) % N_ROW, SEAM)

    barrier = greet([mate, down, up, left, right] + [near_id(q) for q in range(1, 8)] + [far_id(q) for q in range(1, 8)])

    @pl.when(at_seam)
    def _():
        greet([relay_plus, relay_minus, diagonal])

    @pl.when(past_seam)
    def _():
        greet([relay_plus, relay_minus, diagonal_from])

    @pl.when(is_relay)
    def _():
        greet([relay_source, relay_dest])

    extra = jnp.where(at_seam | past_seam, 3, 0) + jnp.where(is_relay, 2, 0)
    pl.semaphore_wait(barrier, 19 + extra)

    halo = (h_send, h_recv)
    corner = remote(area(gext, 4, T, W), corner_in, halo, 0, right)
    cols = remote(area(gext, 4, 0, W), area(right_in, 0, 0, W), halo, 1, right)
    cols2 = remote(area(gext, 4, W, W), area(right_in, 0, W, W), halo, 2, right)
    seam_corner = remote(area(gext, 4, T, W), seam_in, halo, 3, diagonal)
    to_plus = remote(area(gext, 4, 0, W), relay_in, halo, 4, relay_plus)
    to_minus = remote(area(gext, 4, W, W), relay_in, halo, 5, relay_minus)
    relay_upper = remote(relay_in, area(right_in, 0, 0, W), halo, 6, relay_dest)
    relay_lower = remote(relay_in, area(right_in, 0, W, W), halo, 7, relay_dest)
    pieces_r, pieces_l = [], []
    at = 0
    for n, rows in enumerate(PIECES_R):
        pieces_r.append(remote(area(gext, 2, T + at, rows), area(below_r_in, 0, at, rows), (r_send, r_recv), n, down))
        at += rows
    at = 0
    for n, rows in enumerate(PIECES_L):
        sems = (r_send, r_recv)
        pieces_l.append(remote(area(below_sum, 0, at, rows), area(below_l_in, 0, at, rows), sems, len(PIECES_R) + n, down))
        at += rows

    def start(copies):
        for copy in copies:
            copy.start()

    def wait(copies):
        for copy in copies:
            copy.wait()

    swap = remote(part.at[pl.ds(2 * (1 - core), 2)], got0, (m_send, m_recv), 0, mate)
    swap.start()
    when(at_seam, to_plus.start, to_minus.start)
    when(at_seam & has_down, seam_corner.start)
    when(sends_right, corner.start)
    when(has_down, pieces_r[0].start)
    swap.wait()
    for n in range(2):
        acc0[pl.ds(n * W, W), :] = part[2 * core + n] + got0[n]
    spread = [
        remote(acc0.at[block(near_peer(q) * 64, 64)], got1.at[q - 1], (p_send, p_recv), q - 1, near_id(q))
        for q in range(1, 8)
    ]
    start(spread)
    when(sends_right, cols.start)
    below_sum[...] = area(gext, 0, T, W)[...]

    @pl.when(gets_left)
    def _():
        corner.wait_recv()
        below_sum[...] += corner_in[...]

    wait(spread)
    total = acc0[block(near * 64, 64), :]
    for q in range(7):
        total = total + got1[q]
    acc1[...] = total
    when(is_relay & serves_upper, to_plus.wait_recv, relay_upper.start)
    when(is_relay & jnp.logical_not(serves_upper), to_minus.wait_recv, relay_lower.start)
    spread = [
        remote(acc1.at[block(far_peer(q) * 8, 8)], got2.at[q - 1], (x_send, x_recv), q - 1, far_id(q))
        for q in range(1, 8)
    ]
    start(spread)
    wait(spread)
    base1 = core * 512 + near * 64
    own = block(base1 + far * 8, 8)
    total = acc1[block(far * 8, 8), :]
    for q in range(7):
        total = total + got2[q]
    full[own, :] = total
    spread = [remote(full.at[own], full.at[own], (x_send, x_recv), 6 + q, far_id(q)) for q in range(1, 8)]
    start(spread)
    wait(spread)
    own1 = block(base1, 64)
    spread = [remote(full.at[own1], full.at[own1], (p_send, p_recv), 6 + q, near_id(q)) for q in range(1, 8)]
    start(spread)
    when(has_down, *[copy.start for copy in pieces_r[1:] + pieces_l])
    when(sends_right, cols2.start)
    for n in range(T // H):
        out[:, :, pl.ds(n * H, H)] = gext[:, n, pl.ds(0, T), :]
    wait(spread)
    own0 = block(core * 512, 512)
    swap = remote(full.at[own0], full.at[own0], (m_send, m_recv), 1, mate)
    swap.start()
    swap.wait()
    for p in range(2):
        for half in range(2):
            out_p[p, :, pl.ds(H * half, H)] = full[pl.ds((2 * p + half) * W, W), :]

    def add(value, rows, at):
        for n in range(2):
            out[:, pl.ds(0, rows), pl.ds((at + n) * H, H)] += value[:, n]

    @pl.when(has_up)
    def _():
        for copy in pieces_r:
            copy.wait_recv()
        add(below_r_in, W, 2)

    @pl.when(gets_left)
    def _():
        cols.wait_recv()
        cols2.wait_recv()
        add(right_in, T, 0)

    @pl.when(past_seam)
    def _():
        relay_upper.wait_recv()
        relay_lower.wait_recv()
        add(right_in, T, 0)

    @pl.when(has_up)
    def _():
        for copy in pieces_l:
            copy.wait_recv()
        add(below_l_in, W, 0)

    @pl.when(past_seam & has_up)
    def _():
        seam_corner.wait_recv()
        add(seam_in, W, 0)

    when(sends_right, corner.wait_send, cols.wait_send, cols2.wait_send)
    when(has_down, *[copy.wait_send for copy in pieces_r + pieces_l])
    when(at_seam, to_plus.wait_send, to_minus.wait_send)
    when(at_seam & has_down, seam_corner.wait_send)
    when(is_relay & serves_upper, relay_upper.wait_send)
    when(is_relay & jnp.logical_not(serves_upper), relay_lower.wait_send)


PIECES_R = (128, 128)
PIECES_L = (256,)


def back(gext, part):
    dma = pltpu.SemaphoreType.DMA
    vmem = pl.BlockSpec(memory_space=pltpu.VMEM)
    square = VMEM((2, 2, W, H), F32)
    return pl.pallas_call(
        back_kernel,
        out_shape=(jax.ShapeDtypeStruct((2, T, T), F32), jax.ShapeDtypeStruct((2, W, W), F32)),
        in_specs=[vmem, vmem],
        out_specs=(vmem, vmem),
        scratch_shapes=[
            square, VMEM((2, 2, T, H), F32), square, square, square, square, square,
            VMEM((4 * W, H), F32), VMEM((2, W, H), F32), VMEM((2 * W, H), F32),
            VMEM((7, 64, H), F32), VMEM((64, H), F32), VMEM((7, 8, H), F32),
            dma((8,)), dma((8,)), dma((3,)), dma((3,)), dma((2,)), dma((2,)), dma((14,)), dma((14,)), dma((14,)), dma((14,)),
        ],
        compiler_params=pltpu.CompilerParams(
            collective_id=1, has_side_effects=True, vmem_limit_bytes=40 * MIB
        ),
        name="back",
    )(gext, part)


def ahead_kernel(tile, amps, select_t, ext, amps_out, relay_in, amp_buf, h_send, h_recv, t_sem, a_sem):
    row, col, x, y, z, core = place()
    down, up = ((row + 1) % N_ROW, col), ((row + N_ROW - 1) % N_ROW, col)
    to_right, to_left = (row, (col + 1) % N_COL), (row, (col + N_COL - 1) % N_COL)
    at_seam, past_seam = col == SEAM, col == SEAM + 1
    has_down, has_up = row < N_ROW - 1, row > 0
    sends_left = (col > 0) & (col != SEAM + 1)
    gets_right = (col < N_COL - 1) & (col != SEAM)
    x_plus, x_minus = (x + 1) % 4, (x + 3) % 4
    is_relay = (y == AHEAD_Y) & (core == x // 2)
    relay_plus, relay_minus = at_chip(x_plus, AHEAD_Y, z, x_plus // 2), at_chip(x_minus, AHEAD_Y, z, x_minus // 2)
    serves_upper = (x == 3) | (x == 0)
    relay_source = at_chip(jnp.where(serves_upper, x_minus, x_plus), 0, z, 0)
    relay_dest = at_chip(jnp.where(serves_upper, x_plus, x_minus), 3, z, 1)

    lanes = [
        pltpu.make_async_copy(tile.at[:, :, pl.ds(H * n, H)], ext.at[:, n, pl.ds(0, T), :], t_sem.at[n])
        for n in range(T // H)
    ]
    halves = [
        pltpu.make_async_copy(amps.at[:, :, pl.ds(H * n, H)], amp_buf.at[:, n], a_sem.at[n])
        for n in range(2)
    ]
    for copy in lanes + halves:
        copy.start()
    barrier = greet([down, up, to_left, to_right])

    @pl.when(past_seam)
    def _():
        greet([relay_plus, relay_minus, ((row + N_ROW - 1) % N_ROW, SEAM)])

    @pl.when(at_seam)
    def _():
        greet([relay_plus, relay_minus, ((row + 1) % N_ROW, SEAM + 1)])

    @pl.when(is_relay)
    def _():
        greet([relay_source, relay_dest])

    extra = jnp.where(at_seam | past_seam, 3, 0) + jnp.where(is_relay, 2, 0)
    pl.semaphore_wait(barrier, 4 + extra)

    halo = (h_send, h_recv)
    cols = remote(area(ext, 0, 0, T), area(ext, 4, 0, T), halo, 0, to_left)
    rows_l = remote(area(ext, 0, 0, W), area(ext, 0, T, W), halo, 1, up)
    rows_r = remote(area(ext, 2, 0, W), area(ext, 2, T, W), halo, 2, up)
    on_left = remote(area(ext, 0, T, W), area(ext, 4, T, W), halo, 3, to_left)
    seam_corner = remote(area(ext, 0, 0, W), area(ext, 4, T, W), halo, 4, ((row + N_ROW - 1) % N_ROW, SEAM))
    to_plus = remote(area(ext, 0, 0, W), relay_in, halo, 5, relay_plus)
    to_minus = remote(area(ext, 0, W, W), relay_in, halo, 6, relay_minus)
    relay_upper = remote(relay_in, area(ext, 4, 0, W), halo, 7, relay_dest)
    relay_lower = remote(relay_in, area(ext, 4, W, W), halo, 8, relay_dest)

    lanes[0].wait()
    lanes[1].wait()
    when(past_seam, to_plus.start, to_minus.start)
    when(past_seam & has_up, seam_corner.start)
    when(has_up, rows_l.start)
    when(sends_left, cols.start)
    lanes[2].wait()
    lanes[3].wait()
    when(has_up & jnp.logical_not(is_relay), rows_r.start)
    for copy in halves:
        copy.wait()

    def reorder_slot(k, _):
        half = jnp.concatenate(
            [
                jnp.concatenate([amp_buf[k, n, pl.ds(start, H, stride=2), :] for n in range(2)], axis=1)
                for start in range(2)
            ],
            axis=0,
        )
        high, mid = high_low(half)
        low = (half - high.astype(F32) - mid.astype(F32)).astype(BF16)
        chosen = select_t[...].astype(BF16)
        amps_out[k] = dot(high, chosen) + dot(mid, chosen) + dot(low, chosen)
        return 0

    lax.fori_loop(0, amps.shape[0], reorder_slot, 0)
    when(is_relay & serves_upper, to_plus.wait_recv, relay_upper.start)
    when(is_relay & jnp.logical_not(serves_upper), to_minus.wait_recv, relay_lower.start)
    when(is_relay & has_up, rows_r.start)
    when(has_down, rows_l.wait_recv)
    when(has_down & sends_left, on_left.start)
    when(has_down, rows_r.wait_recv)
    when(gets_right, cols.wait_recv)
    when(at_seam, relay_upper.wait_recv, relay_lower.wait_recv)
    when(gets_right & has_down, on_left.wait_recv)
    when(at_seam & has_down, seam_corner.wait_recv)
    when(sends_left, cols.wait_send)
    when(has_up, rows_l.wait_send, rows_r.wait_send)
    when(has_down & sends_left, on_left.wait_send)
    when(past_seam, to_plus.wait_send, to_minus.wait_send)
    when(past_seam & has_up, seam_corner.wait_send)
    when(is_relay & serves_upper, relay_upper.wait_send)
    when(is_relay & jnp.logical_not(serves_upper), relay_lower.wait_send)


def ahead(tile, amps):
    n = np.arange(H)
    select = np.zeros((W, W), np.float32)
    select[2 * n, n] = 1.0
    select[2 * n + 1, H + n] = 1.0
    dma = pltpu.SemaphoreType.DMA
    vmem = pl.BlockSpec(memory_space=pltpu.VMEM)
    any_spec = pl.BlockSpec(memory_space=pl.ANY)
    return pl.pallas_call(
        ahead_kernel,
        out_shape=(jax.ShapeDtypeStruct(EXT, F32), jax.ShapeDtypeStruct(amps.shape, F32)),
        in_specs=[any_spec, any_spec, vmem],
        out_specs=(vmem, vmem),
        scratch_shapes=[
            VMEM((2, 2, W, H), F32), VMEM((amps.shape[0], 2, W, H), F32),
            dma((9,)), dma((9,)), dma((T // H,)), dma((2,)),
        ],
        compiler_params=pltpu.CompilerParams(
            collective_id=0, has_side_effects=True, vmem_limit_bytes=40 * MIB
        ),
        name="ahead",
    )(tile, amps, jnp.asarray(select))


def on_device(object_tile, probe, amplitudes, positions, counts):
    ext, amps = ahead(object_tile, amplitudes[0, 0])
    gext, part = run_slots(positions[0, 0].T, counts, ext, amps, probe)
    return back(gext, part)


def solution(mesh):
    in_specs = (
        P(None, "row", "col"),
        P(),
        P("row", "col", None, None, None),
        P("row", "col", None, None),
        P("row", None),
    )
    out_specs = (P(None, "row", "col"), P())
    return jax.shard_map(
        on_device, mesh=mesh, in_specs=in_specs, out_specs=out_specs, check_vma=False
    )
```

time: 136 us -> 122 us (0.90)
  Pallas kernels: 121 us -> 113 us
  local copies, waits for them, and re-layouts: 13.4 us -> 6.86 us
    pallas_call x3, Pallas kernels: 121 us -> 113 us  [the longest x1 61.7 us: back(): pl.pallas_call(back_kernel, out_shape=(jax.ShapeDtypeStruct((2, T, T), F3...]
    unnamed x18 -> x16, local copies, waits for them, and re-layouts: 12 us -> 6.86 us
where the time goes in v3:
time: 122 us; the launch traced here: 120 us
  Pallas kernels  113 us (93%)
  local copies, waits for them, and re-layouts  6.86 us (6%)
    pallas_call x1, Pallas kernels, back(): pl.pallas_call(back_kernel, out_shape=(jax.ShapeDtypeStruct((2, T, T), F3...  61.7 us
    pallas_call x1, Pallas kernels, ahead(): pl.pallas_call(ahead_kernel, out_shape=(jax.ShapeDtypeStruct(EXT, F32), j...  28.6 us
    pallas_call x1, Pallas kernels, run_slots(): pl.pallas_call(slots_kernel, out_shape=(jax.ShapeDtypeStruct(EXT, F32), j...  22.3 us
    unnamed x16, local copies, waits for them, and re-layouts  6.86 us

profile of v3, /device:TPU:1, one launch (start us, length us, event | category | flops | bytes accessed | tf_op | source)
XLA Modules:
  0.0 120.2 jit_solution(2723272107200405811)
XLA Ops:
  0.6 0.0 copy-start.6
  0.6 0.0 copy-start.5
  0.7 0.0 copy-start
  0.7 2.2 %copy-done = f32[1,1,16,256,256]{4,3,2,1,0:T(8,128)S(1)} copy-done((f32[1,1,16,256,256]{4,3,2,1,0:T(8,128)S(1)}, f32[1,1,16,256,256]{4,3,2,1,0:T(8,128)}, u32[]{:S(2)}) %copy-start) | copy-done | bytes 4194328
  2.9 0.0 copy-start.1
  2.9 1.6 %copy-done.1 = f32[2,512,512]{2,1,0:T(8,128)S(1)} copy-done((f32[2,512,512]{2,1,0:T(8,128)S(1)}, f32[2,512,512]{2,1,0:T(8,128)}, u32[]{:S(2)}) %copy-start.1) | copy-done | bytes 2097176
  4.4 0.0 copy-start.4
  4.4 0.9 copy-done.4
  5.4 0.0 copy-start.2
  5.4 0.0 copy-start.3
  5.4 28.6 %ahead.1 = (f32[2,6,768,128]{3,2,1,0:T(8,128)}, f32[16,256,256]{2,1,0:T(8,128)S(1)}) custom-call(f32[2,512,512]{2,1,0:T(8,128)S(1)} %copy-done.1, f32[16,256,256]{2,1,0:T(8,128)S(1)} %bitcast.4, f32[256,256]{1,0:T(8,128)S(1)} %copy-done.4), custom_call_target="tpu_custom_call" | custom-call | tf_op jit(solution)/shard_map/ahead/pallas_call | solution.py:592
  34.0 0.0 copy-done.6
  34.1 0.0 copy-done.5
  34.1 0.0 copy-done.2
  34.1 0.0 copy-done.3
  34.1 22.3 %slots.1 = (f32[2,6,768,128]{3,2,1,0:T(8,128)S(1)}, f32[4,256,128]{2,1,0:T(8,128)S(1)}) custom-call(s32[2,16]{1,0:T(2,128)S(1)} %bitcast.5, s32[1,16]{1,0:T(1,128)S(1)} %copy-done.6, f32[2,6,768,128]{3,2,1,0:T(8,128)} %get-tuple-element.6.ext, f32[16,256,256]{2,1,0:T(8,128)S(1)} %get-tuple-element.7.amps, f32[2,256,256]{2,1,0:T(8,128)S(1)} %copy-done.3, ...), custom_call_target="tpu_custom_call" | custom-call | tf_op jit(solution)/shard_map/slots/pallas_call | solution.py:213
  56.4 61.7 %back.1 = (f32[2,512,512]{2,1,0:T(8,128)S(1)}, f32[2,256,256]{2,1,0:T(8,128)S(1)}) custom-call(f32[2,6,768,128]{3,2,1,0:T(8,128)S(1)} %get-tuple-element.8.gext, f32[4,256,128]{2,1,0:T(8,128)S(1)} %get-tuple-element.9.part), custom_call_target="tpu_custom_call" | custom-call | tf_op jit(solution)/shard_map/back/pallas_call | solution.py:467
  118.0 1.3 %copy.11 = f32[2,512,512]{2,1,0:T(8,128)} copy(f32[2,512,512]{2,1,0:T(8,128)S(1)} %get-tuple-element.12) | data formatting | bytes 4194304
  119.4 0.8 copy.12
Async XLA Ops:
  0.6 33.4 %copy-start.6 = (s32[1,16]{1,0:T(1,128)S(1)}, s32[1,16]{1,0:T(1,128)}, u32[]{:S(2)}) copy-start(s32[1,16]{1,0:T(1,128)} %counts.1) | copy-start | bytes 196
  0.6 33.4 %copy-start.5 = (s32[1,1,16,2]{2,3,1,0:T(2,128)S(1)}, s32[1,1,16,2]{2,3,1,0:T(2,128)}, u32[]{:S(2)}) copy-start(s32[1,1,16,2]{2,3,1,0:T(2,128)} %param.10) | copy-start | bytes 388
  0.7 2.2 %copy-start = (f32[1,1,16,256,256]{4,3,2,1,0:T(8,128)S(1)}, f32[1,1,16,256,256]{4,3,2,1,0:T(8,128)}, u32[]{:S(2)}) copy-start(f32[1,1,16,256,256]{4,3,2,1,0:T(8,128)} %param.9) | copy-start | bytes 12582916
  2.9 1.6 %copy-start.1 = (f32[2,512,512]{2,1,0:T(8,128)S(1)}, f32[2,512,512]{2,1,0:T(8,128)}, u32[]{:S(2)}) copy-start(f32[2,512,512]{2,1,0:T(8,128)} %tile.1) | copy-start | bytes 6291460
  4.4 0.9 copy-start.4
  5.4 28.7 %copy-start.2 = (f32[4,256,256]{2,1,0:T(8,128)S(1)}, f32[4,256,256]{2,1,0:T(8,128)}, u32[]{:S(2)}) copy-start(f32[4,256,256]{2,1,0:T(8,128)} %constant.5.clone.table) | copy-start | bytes 3145732
  5.4 28.7 %copy-start.3 = (f32[2,256,256]{2,1,0:T(8,128)S(1)}, f32[2,256,256]{2,1,0:T(8,128)}, u32[]{:S(2)}) copy-start(f32[2,256,256]{2,1,0:T(8,128)} %probe.1) | copy-start | bytes 1572868

commit v4 on v3

--- a/solution.py
+++ b/solution.py
@@ -20,7 +20,7 @@
 MESH = pl.DeviceIdType.MESH
 N_ROW, N_COL = 8, 16
 SEAM = 7
-AHEAD_Y, BACK_Y = 0, 3
+BACK_Y = 3
 EXT = (2, TILES, T + W, H)
 MIB = 1024 * 1024
 
@@ -225,7 +225,7 @@
             VMEM((U, W, W), F32),
             pltpu.SemaphoreType.DMA((2,)),
         ],
-        compiler_params=pltpu.CompilerParams(vmem_limit_bytes=40 * MIB),
+        compiler_params=pltpu.CompilerParams(vmem_limit_bytes=28 * MIB),
         name="slots",
     )(own_pos, counts, ext, amps, probe, jnp.asarray(tables()))
 
@@ -382,8 +382,6 @@
     for q in range(7):
         total = total + got1[q]
     acc1[...] = total
-    when(is_relay & serves_upper, to_plus.wait_recv, relay_upper.start)
-    when(is_relay & jnp.logical_not(serves_upper), to_minus.wait_recv, relay_lower.start)
     spread = [
         remote(acc1.at[block(far_peer(q) * 8, 8)], got2.at[q - 1], (x_send, x_recv), q - 1, far_id(q))
         for q in range(1, 8)
@@ -402,6 +400,8 @@
     own1 = block(base1, 64)
     spread = [remote(full.at[own1], full.at[own1], (p_send, p_recv), 6 + q, near_id(q)) for q in range(1, 8)]
     start(spread)
+    when(is_relay & serves_upper, to_plus.wait_recv, relay_upper.start)
+    when(is_relay & jnp.logical_not(serves_upper), to_minus.wait_recv, relay_lower.start)
     when(has_down, *[copy.start for copy in pieces_r[1:] + pieces_l])
     when(sends_right, cols2.start)
     for n in range(T // H):
@@ -476,13 +476,13 @@
             dma((8,)), dma((8,)), dma((3,)), dma((3,)), dma((2,)), dma((2,)), dma((14,)), dma((14,)), dma((14,)), dma((14,)),
         ],
         compiler_params=pltpu.CompilerParams(
-            collective_id=1, has_side_effects=True, vmem_limit_bytes=40 * MIB
+            collective_id=1, has_side_effects=True, vmem_limit_bytes=24 * MIB
         ),
         name="back",
     )(gext, part)
 
 
-def ahead_kernel(tile, amps, select_t, ext, amps_out, relay_in, amp_buf, h_send, h_recv, t_sem, a_sem):
+def ahead_kernel(tile, amps, ext, amps_out, relay_in, amp_buf, h_send, h_recv, t_sem, a_sem):
     row, col, x, y, z, core = place()
     down, up = ((row + 1) % N_ROW, col), ((row + N_ROW - 1) % N_ROW, col)
     to_right, to_left = (row, (col + 1) % N_COL), (row, (col + N_COL - 1) % N_COL)
@@ -490,12 +490,9 @@
     has_down, has_up = row < N_ROW - 1, row > 0
     sends_left = (col > 0) & (col != SEAM + 1)
     gets_right = (col < N_COL - 1) & (col != SEAM)
-    x_plus, x_minus = (x + 1) % 4, (x + 3) % 4
-    is_relay = (y == AHEAD_Y) & (core == x // 2)
-    relay_plus, relay_minus = at_chip(x_plus, AHEAD_Y, z, x_plus // 2), at_chip(x_minus, AHEAD_Y, z, x_minus // 2)
-    serves_upper = (x == 3) | (x == 0)
-    relay_source = at_chip(jnp.where(serves_upper, x_minus, x_plus), 0, z, 0)
-    relay_dest = at_chip(jnp.where(serves_upper, x_plus, x_minus), 3, z, 1)
+    source, target = at_chip((x + 2) % 4, 0, z, 0), at_chip((x + 2) % 4, 3, z, 1)
+    is_relay = (x < 2) & (y < 3) & (core == 1)
+    relay_target = at_chip(x, 3, z, 1)
 
     lanes = [
         pltpu.make_async_copy(tile.at[:, :, pl.ds(H * n, H)], ext.at[:, n, pl.ds(0, T), :], t_sem.at[n])
@@ -511,17 +508,17 @@
 
     @pl.when(past_seam)
     def _():
-        greet([relay_plus, relay_minus, ((row + N_ROW - 1) % N_ROW, SEAM)])
+        greet([at_chip((x + 2) % 4, q, z, 1) for q in range(3)] + [((row + N_ROW - 1) % N_ROW, SEAM)])
 
     @pl.when(at_seam)
     def _():
-        greet([relay_plus, relay_minus, ((row + 1) % N_ROW, SEAM + 1)])
+        greet([at_chip(x, q, z, 1) for q in range(3)] + [((row + 1) % N_ROW, SEAM + 1)])
 
     @pl.when(is_relay)
     def _():
-        greet([relay_source, relay_dest])
-
-    extra = jnp.where(at_seam | past_seam, 3, 0) + jnp.where(is_relay, 2, 0)
+        greet([source, relay_target])
+
+    extra = jnp.where(at_seam | past_seam, 4, 0) + jnp.where(is_relay, 2, 0)
     pl.semaphore_wait(barrier, 4 + extra)
 
     halo = (h_send, h_recv)
@@ -530,22 +527,30 @@
     rows_r = remote(area(ext, 2, 0, W), area(ext, 2, T, W), halo, 2, up)
     on_left = remote(area(ext, 0, T, W), area(ext, 4, T, W), halo, 3, to_left)
     seam_corner = remote(area(ext, 0, 0, W), area(ext, 4, T, W), halo, 4, ((row + N_ROW - 1) % N_ROW, SEAM))
-    to_plus = remote(area(ext, 0, 0, W), relay_in, halo, 5, relay_plus)
-    to_minus = remote(area(ext, 0, W, W), relay_in, halo, 6, relay_minus)
-    relay_upper = remote(relay_in, area(ext, 4, 0, W), halo, 7, relay_dest)
-    relay_lower = remote(relay_in, area(ext, 4, W, W), halo, 8, relay_dest)
+    parts = [
+        remote(area(ext, 0, H * q, H), relay_in, halo, 5 + q, at_chip((x + 2) % 4, q, z, 1)) for q in range(3)
+    ]
+    parts.append(remote(area(ext, 0, 3 * H, H), area(ext, 4, 3 * H, H), halo, 8, target))
+    arrived = remote(relay_in, relay_in, halo, 5 + y % 3, relay_target)
+    passed = remote(relay_in, area(ext, 4, H * (y % 3), H), halo, 9 + y % 3, relay_target)
+    got = [remote(relay_in, area(ext, 4, H * q, H), halo, 9 + q, relay_target) for q in range(3)]
 
     lanes[0].wait()
     lanes[1].wait()
-    when(past_seam, to_plus.start, to_minus.start)
+    when(past_seam, *[copy.start for copy in parts])
     when(past_seam & has_up, seam_corner.start)
     when(has_up, rows_l.start)
     when(sends_left, cols.start)
     lanes[2].wait()
     lanes[3].wait()
-    when(has_up & jnp.logical_not(is_relay), rows_r.start)
+    when(has_up, rows_r.start)
     for copy in halves:
         copy.wait()
+
+    source_at = lax.broadcasted_iota(jnp.int32, (W, W), 0)
+    place_at = lax.broadcasted_iota(jnp.int32, (W, W), 1)
+    odd = (place_at >= H).astype(jnp.int32)
+    chosen = (source_at == 2 * (place_at - H * odd) + odd).astype(F32).astype(BF16)
 
     def reorder_slot(k, _):
         half = jnp.concatenate(
@@ -557,52 +562,44 @@
         )
         high, mid = high_low(half)
         low = (half - high.astype(F32) - mid.astype(F32)).astype(BF16)
-        chosen = select_t[...].astype(BF16)
         amps_out[k] = dot(high, chosen) + dot(mid, chosen) + dot(low, chosen)
         return 0
 
     lax.fori_loop(0, amps.shape[0], reorder_slot, 0)
-    when(is_relay & serves_upper, to_plus.wait_recv, relay_upper.start)
-    when(is_relay & jnp.logical_not(serves_upper), to_minus.wait_recv, relay_lower.start)
-    when(is_relay & has_up, rows_r.start)
+    when(is_relay, arrived.wait_recv, passed.start)
     when(has_down, rows_l.wait_recv)
     when(has_down & sends_left, on_left.start)
     when(has_down, rows_r.wait_recv)
     when(gets_right, cols.wait_recv)
-    when(at_seam, relay_upper.wait_recv, relay_lower.wait_recv)
+    when(at_seam, *[copy.wait_recv for copy in got], parts[3].wait_recv)
     when(gets_right & has_down, on_left.wait_recv)
     when(at_seam & has_down, seam_corner.wait_recv)
     when(sends_left, cols.wait_send)
     when(has_up, rows_l.wait_send, rows_r.wait_send)
     when(has_down & sends_left, on_left.wait_send)
-    when(past_seam, to_plus.wait_send, to_minus.wait_send)
+    when(past_seam, *[copy.wait_send for copy in parts])
     when(past_seam & has_up, seam_corner.wait_send)
-    when(is_relay & serves_upper, relay_upper.wait_send)
-    when(is_relay & jnp.logical_not(serves_upper), relay_lower.wait_send)
+    when(is_relay, passed.wait_send)
 
 
 def ahead(tile, amps):
-    n = np.arange(H)
-    select = np.zeros((W, W), np.float32)
-    select[2 * n, n] = 1.0
-    select[2 * n + 1, H + n] = 1.0
     dma = pltpu.SemaphoreType.DMA
     vmem = pl.BlockSpec(memory_space=pltpu.VMEM)
-    any_spec = pl.BlockSpec(memory_space=pl.ANY)
+    hbm = pl.BlockSpec(memory_space=pltpu.HBM)
     return pl.pallas_call(
         ahead_kernel,
         out_shape=(jax.ShapeDtypeStruct(EXT, F32), jax.ShapeDtypeStruct(amps.shape, F32)),
-        in_specs=[any_spec, any_spec, vmem],
+        in_specs=[hbm, hbm],
         out_specs=(vmem, vmem),
         scratch_shapes=[
-            VMEM((2, 2, W, H), F32), VMEM((amps.shape[0], 2, W, H), F32),
-            dma((9,)), dma((9,)), dma((T // H,)), dma((2,)),
+            VMEM((2, 2, H, H), F32), VMEM((amps.shape[0], 2, W, H), F32),
+            dma((12,)), dma((12,)), dma((T // H,)), dma((2,)),
         ],
         compiler_params=pltpu.CompilerParams(
-            collective_id=0, has_side_effects=True, vmem_limit_bytes=40 * MIB
+            collective_id=0, has_side_effects=True, vmem_limit_bytes=24 * MIB
         ),
         name="ahead",
-    )(tile, amps, jnp.asarray(select))
+    )(tile, amps)
 
 
 def on_device(object_tile, probe, amplitudes, positions, counts):

time: 122 us -> 110 us (0.902)
  the two profiles are of different devices: /device:TPU:1 before, /device:TPU:61 now
where the time goes in v4:
time: 110 us
  Pallas kernels  104 us (95%)
  local copies, waits for them, and re-layouts  5.91 us (5%)
    pallas_call x1, Pallas kernels, back(): pl.pallas_call(back_kernel, out_shape=(jax.ShapeDtypeStruct((2, T, T), F3...  76.3 us
    pallas_call x1, Pallas kernels, ahead(): pl.pallas_call(ahead_kernel, out_shape=(jax.ShapeDtypeStruct(EXT, F32), j...  26.2 us
    unnamed x14, local copies, waits for them, and re-layouts  5.91 us

profile of v4, /device:TPU:61, one launch (start us, length us, event | category | flops | bytes accessed | tf_op | source)
XLA Modules:
  0.0 110.3 jit_solution(847155223408428880)
XLA Ops:
  0.6 0.0 copy-start.5
  0.6 0.0 copy-start.4
  0.7 0.0 copy-start
  0.7 2.2 %copy-done = f32[1,1,16,256,256]{4,3,2,1,0:T(8,128)S(1)} copy-done((f32[1,1,16,256,256]{4,3,2,1,0:T(8,128)S(1)}, f32[1,1,16,256,256]{4,3,2,1,0:T(8,128)}, u32[]{:S(2)}) %copy-start) | copy-done | bytes 4194328
  2.9 0.0 copy-start.1
  2.9 1.6 %copy-done.1 = f32[2,512,512]{2,1,0:T(8,128)S(1)} copy-done((f32[2,512,512]{2,1,0:T(8,128)S(1)}, f32[2,512,512]{2,1,0:T(8,128)}, u32[]{:S(2)}) %copy-start.1) | copy-done | bytes 2097176
  4.4 0.0 copy-start.2
  4.4 0.0 copy-start.3
  4.4 26.2 %ahead.1 = (f32[2,6,768,128]{3,2,1,0:T(8,128)S(1)}, f32[16,256,256]{2,1,0:T(8,128)S(1)}) custom-call(f32[2,512,512]{2,1,0:T(8,128)S(1)} %copy-done.1, f32[16,256,256]{2,1,0:T(8,128)S(1)} %bitcast.4), custom_call_target="tpu_custom_call" | custom-call | tf_op jit(solution)/shard_map/ahead/pallas_call | solution.py:589
  30.7 0.0 copy-done.5
  30.7 0.0 copy-done.4
  30.7 0.0 copy-done.2
  30.7 0.0 copy-done.3
  30.7 1.1 slots.1
  31.8 76.3 %back.1 = (f32[2,512,512]{2,1,0:T(8,128)S(1)}, f32[2,256,256]{2,1,0:T(8,128)S(1)}) custom-call(f32[2,6,768,128]{3,2,1,0:T(8,128)S(1)} %get-tuple-element.8.gext, f32[4,256,128]{2,1,0:T(8,128)S(1)} %get-tuple-element.9.part), custom_call_target="tpu_custom_call" | custom-call | tf_op jit(solution)/shard_map/back/pallas_call | solution.py:467
  108.2 1.3 %copy.10 = f32[2,512,512]{2,1,0:T(8,128)} copy(f32[2,512,512]{2,1,0:T(8,128)S(1)} %get-tuple-element.12) | data formatting | bytes 4194304
  109.5 0.8 copy.11
Async XLA Ops:
  0.6 30.0 %copy-start.5 = (s32[1,16]{1,0:T(1,128)S(1)}, s32[1,16]{1,0:T(1,128)}, u32[]{:S(2)}) copy-start(s32[1,16]{1,0:T(1,128)} %counts.1) | copy-start | bytes 196
  0.6 30.0 %copy-start.4 = (s32[1,1,16,2]{2,3,1,0:T(2,128)S(1)}, s32[1,1,16,2]{2,3,1,0:T(2,128)}, u32[]{:S(2)}) copy-start(s32[1,1,16,2]{2,3,1,0:T(2,128)} %param.9) | copy-start | bytes 388
  0.7 2.2 %copy-start = (f32[1,1,16,256,256]{4,3,2,1,0:T(8,128)S(1)}, f32[1,1,16,256,256]{4,3,2,1,0:T(8,128)}, u32[]{:S(2)}) copy-start(f32[1,1,16,256,256]{4,3,2,1,0:T(8,128)} %param.8) | copy-start | bytes 12582916
  2.9 1.6 %copy-start.1 = (f32[2,512,512]{2,1,0:T(8,128)S(1)}, f32[2,512,512]{2,1,0:T(8,128)}, u32[]{:S(2)}) copy-start(f32[2,512,512]{2,1,0:T(8,128)} %tile.1) | copy-start | bytes 6291460
  4.4 26.2 %copy-start.2 = (f32[4,256,256]{2,1,0:T(8,128)S(1)}, f32[4,256,256]{2,1,0:T(8,128)}, u32[]{:S(2)}) copy-start(f32[4,256,256]{2,1,0:T(8,128)} %constant.2.clone.table) | copy-start | bytes 3145732
  4.4 26.3 %copy-start.3 = (f32[2,256,256]{2,1,0:T(8,128)S(1)}, f32[2,256,256]{2,1,0:T(8,128)}, u32[]{:S(2)}) copy-start(f32[2,256,256]{2,1,0:T(8,128)} %probe.1) | copy-start | bytes 1572868

commit v5 on v4

--- a/solution.py
+++ b/solution.py
@@ -20,7 +20,7 @@
 MESH = pl.DeviceIdType.MESH
 N_ROW, N_COL = 8, 16
 SEAM = 7
-BACK_Y = 3
+
 EXT = (2, TILES, T + W, H)
 MIB = 1024 * 1024
 
@@ -270,6 +270,10 @@
     return ref.at[:, pl.ds(tile, 2), pl.ds(row, rows), :]
 
 
+def at_rows(ref, tile, row, rows):
+    return ref.at[:, pl.ds(tile, 2), block(row, rows), :]
+
+
 def back_kernel(
     gext, part, out, out_p, corner_in, right_in, below_l_in, below_r_in, seam_in, relay_in, below_sum,
     full, got0, acc0, got1, acc1, got2,
@@ -297,16 +301,15 @@
         return at_chip(n // 4 + place_in_pair * (3 - 2 * (n // 4)), y, n % 4, core)
 
     at_seam, past_seam = col == SEAM, col == SEAM + 1
-    x_plus, x_minus = (x + 1) % 4, (x + 3) % 4
-    is_relay = (y == BACK_Y) & (core == x // 2)
+    side, idle_side = (5 - x) % 4, (3 - x) % 4
+    half, other_half = jnp.where(x == 0, 0, W), jnp.where(x == 0, W, 0)
+    relays_half, relays_quarter = (y == 3) & (core == 0) & (x < 2), (y == 3) & (x >= 2)
+    is_relay = relays_half | relays_quarter
+    source = at_chip(jnp.where(x < 2, 1 - x, 3 - x), 3, z, 1)
+    target = at_chip(jnp.where(x < 2, 3 - x, 5 - x), 0, z, 0)
     has_down, has_up = row < N_ROW - 1, row > 0
     sends_right = (col < N_COL - 1) & (col != SEAM)
     gets_left = (col > 0) & (col != SEAM + 1)
-    relay_plus = at_chip(x_plus, BACK_Y, z, x_plus // 2)
-    relay_minus = at_chip(x_minus, BACK_Y, z, x_minus // 2)
-    serves_upper = (x == 1) | (x == 2)
-    relay_source = at_chip(jnp.where(serves_upper, x_minus, x_plus), 3, z, 1)
-    relay_dest = at_chip(jnp.where(serves_upper, x_plus, x_minus), 0, z, 0)
     diagonal = ((row + 1) % N_ROW, SEAM + 1)
     diagonal_from = ((row + N_ROW - 1) % N_ROW, SEAM)
 
@@ -314,17 +317,17 @@
 
     @pl.when(at_seam)
     def _():
-        greet([relay_plus, relay_minus, diagonal])
+        greet([at_chip(side, 3, z, 0)] + [at_chip(idle_side, 3, z, n) for n in range(2)] + [diagonal])
 
     @pl.when(past_seam)
     def _():
-        greet([relay_plus, relay_minus, diagonal_from])
+        greet([at_chip(idle_side, 3, z, 0)] + [at_chip(side, 3, z, n) for n in range(2)] + [diagonal_from])
 
     @pl.when(is_relay)
     def _():
-        greet([relay_source, relay_dest])
-
-    extra = jnp.where(at_seam | past_seam, 3, 0) + jnp.where(is_relay, 2, 0)
+        greet([source, target])
+
+    extra = jnp.where(at_seam | past_seam, 4, 0) + jnp.where(is_relay, 2, 0)
     pl.semaphore_wait(barrier, 19 + extra)
 
     halo = (h_send, h_recv)
@@ -332,10 +335,16 @@
     cols = remote(area(gext, 4, 0, W), area(right_in, 0, 0, W), halo, 1, right)
     cols2 = remote(area(gext, 4, W, W), area(right_in, 0, W, W), halo, 2, right)
     seam_corner = remote(area(gext, 4, T, W), seam_in, halo, 3, diagonal)
-    to_plus = remote(area(gext, 4, 0, W), relay_in, halo, 4, relay_plus)
-    to_minus = remote(area(gext, 4, W, W), relay_in, halo, 5, relay_minus)
-    relay_upper = remote(relay_in, area(right_in, 0, 0, W), halo, 6, relay_dest)
-    relay_lower = remote(relay_in, area(right_in, 0, W, W), halo, 7, relay_dest)
+    quarter_in = relay_in.at[:, :, pl.ds(0, H), :]
+    parts = [remote(at_rows(gext, 4, half, W), relay_in, halo, 4, at_chip(side, 3, z, 0))]
+    for n in range(2):
+        parts.append(remote(at_rows(gext, 4, other_half + H * n, H), quarter_in, halo, 5 + n, at_chip(idle_side, 3, z, n)))
+    half_in = remote(relay_in, relay_in, halo, 4, target)
+    half_on = remote(relay_in, at_rows(right_in, 0, jnp.where(x == 1, 0, W), W), halo, 7, target)
+    quarter = remote(quarter_in, quarter_in, halo, 5 + core, target)
+    quarter_on = remote(quarter_in, at_rows(right_in, 0, jnp.where(x == 3, W, 0) + H * core, H), halo, 8 + core, target)
+    got = [remote(relay_in, area(right_in, 0, 0, W), halo, 7, target)]
+    got += [remote(quarter_in, area(right_in, 0, 0, H), halo, 8 + n, target) for n in range(2)]
     pieces_r, pieces_l = [], []
     at = 0
     for n, rows in enumerate(PIECES_R):
@@ -357,7 +366,7 @@
 
     swap = remote(part.at[pl.ds(2 * (1 - core), 2)], got0, (m_send, m_recv), 0, mate)
     swap.start()
-    when(at_seam, to_plus.start, to_minus.start)
+    when(at_seam, parts[1].start, parts[2].start, parts[0].start)
     when(at_seam & has_down, seam_corner.start)
     when(sends_right, corner.start)
     when(has_down, pieces_r[0].start)
@@ -394,14 +403,14 @@
     for q in range(7):
         total = total + got2[q]
     full[own, :] = total
+    when(relays_quarter, quarter.wait_recv, quarter_on.start)
     spread = [remote(full.at[own], full.at[own], (x_send, x_recv), 6 + q, far_id(q)) for q in range(1, 8)]
     start(spread)
     wait(spread)
     own1 = block(base1, 64)
     spread = [remote(full.at[own1], full.at[own1], (p_send, p_recv), 6 + q, near_id(q)) for q in range(1, 8)]
     start(spread)
-    when(is_relay & serves_upper, to_plus.wait_recv, relay_upper.start)
-    when(is_relay & jnp.logical_not(serves_upper), to_minus.wait_recv, relay_lower.start)
+    when(relays_half, half_in.wait_recv, half_on.start)
     when(has_down, *[copy.start for copy in pieces_r[1:] + pieces_l])
     when(sends_right, cols2.start)
     for n in range(T // H):
@@ -433,8 +442,8 @@
 
     @pl.when(past_seam)
     def _():
-        relay_upper.wait_recv()
-        relay_lower.wait_recv()
+        for copy in got:
+            copy.wait_recv()
         add(right_in, T, 0)
 
     @pl.when(has_up)
@@ -450,10 +459,10 @@
 
     when(sends_right, corner.wait_send, cols.wait_send, cols2.wait_send)
     when(has_down, *[copy.wait_send for copy in pieces_r + pieces_l])
-    when(at_seam, to_plus.wait_send, to_minus.wait_send)
+    when(at_seam, *[copy.wait_send for copy in parts])
     when(at_seam & has_down, seam_corner.wait_send)
-    when(is_relay & serves_upper, relay_upper.wait_send)
-    when(is_relay & jnp.logical_not(serves_upper), relay_lower.wait_send)
+    when(relays_quarter, quarter_on.wait_send)
+    when(relays_half, half_on.wait_send)
 
 
 PIECES_R = (128, 128)
@@ -473,7 +482,7 @@
             square, VMEM((2, 2, T, H), F32), square, square, square, square, square,
             VMEM((4 * W, H), F32), VMEM((2, W, H), F32), VMEM((2 * W, H), F32),
             VMEM((7, 64, H), F32), VMEM((64, H), F32), VMEM((7, 8, H), F32),
-            dma((8,)), dma((8,)), dma((3,)), dma((3,)), dma((2,)), dma((2,)), dma((14,)), dma((14,)), dma((14,)), dma((14,)),
+            dma((10,)), dma((10,)), dma((3,)), dma((3,)), dma((2,)), dma((2,)), dma((14,)), dma((14,)), dma((14,)), dma((14,)),
         ],
         compiler_params=pltpu.CompilerParams(
             collective_id=1, has_side_effects=True, vmem_limit_bytes=24 * MIB
@@ -490,9 +499,12 @@
     has_down, has_up = row < N_ROW - 1, row > 0
     sends_left = (col > 0) & (col != SEAM + 1)
     gets_right = (col < N_COL - 1) & (col != SEAM)
-    source, target = at_chip((x + 2) % 4, 0, z, 0), at_chip((x + 2) % 4, 3, z, 1)
-    is_relay = (x < 2) & (y < 3) & (core == 1)
-    relay_target = at_chip(x, 3, z, 1)
+    side, idle_side = (5 - x) % 4, (3 - x) % 4
+    half, other_half = jnp.where(x == 2, 0, W), jnp.where(x == 2, W, 0)
+    relays_half, relays_quarter = (y == 0) & (core == 1) & (x >= 2), (y == 0) & (x < 2)
+    is_relay = relays_half | relays_quarter
+    source = at_chip(jnp.where(x >= 2, 5 - x, 3 - x), 0, z, 0)
+    target = at_chip(jnp.where(x >= 2, 3 - x, 1 - x), 3, z, 1)
 
     lanes = [
         pltpu.make_async_copy(tile.at[:, :, pl.ds(H * n, H)], ext.at[:, n, pl.ds(0, T), :], t_sem.at[n])
@@ -508,15 +520,17 @@
 
     @pl.when(past_seam)
     def _():
-        greet([at_chip((x + 2) % 4, q, z, 1) for q in range(3)] + [((row + N_ROW - 1) % N_ROW, SEAM)])
+        greet([at_chip(side, 0, z, 1)] + [at_chip(idle_side, 0, z, n) for n in range(2)])
+        greet([((row + N_ROW - 1) % N_ROW, SEAM)])
 
     @pl.when(at_seam)
     def _():
-        greet([at_chip(x, q, z, 1) for q in range(3)] + [((row + 1) % N_ROW, SEAM + 1)])
+        greet([at_chip((3 - x) % 4, 0, z, 1)] + [at_chip((1 - x) % 4, 0, z, n) for n in range(2)])
+        greet([((row + 1) % N_ROW, SEAM + 1)])
 
     @pl.when(is_relay)
     def _():
-        greet([source, relay_target])
+        greet([source, target])
 
     extra = jnp.where(at_seam | past_seam, 4, 0) + jnp.where(is_relay, 2, 0)
     pl.semaphore_wait(barrier, 4 + extra)
@@ -527,17 +541,20 @@
     rows_r = remote(area(ext, 2, 0, W), area(ext, 2, T, W), halo, 2, up)
     on_left = remote(area(ext, 0, T, W), area(ext, 4, T, W), halo, 3, to_left)
     seam_corner = remote(area(ext, 0, 0, W), area(ext, 4, T, W), halo, 4, ((row + N_ROW - 1) % N_ROW, SEAM))
-    parts = [
-        remote(area(ext, 0, H * q, H), relay_in, halo, 5 + q, at_chip((x + 2) % 4, q, z, 1)) for q in range(3)
-    ]
-    parts.append(remote(area(ext, 0, 3 * H, H), area(ext, 4, 3 * H, H), halo, 8, target))
-    arrived = remote(relay_in, relay_in, halo, 5 + y % 3, relay_target)
-    passed = remote(relay_in, area(ext, 4, H * (y % 3), H), halo, 9 + y % 3, relay_target)
-    got = [remote(relay_in, area(ext, 4, H * q, H), halo, 9 + q, relay_target) for q in range(3)]
+    quarter_in = relay_in.at[:, :, pl.ds(0, H), :]
+    parts = [remote(at_rows(ext, 0, half, W), relay_in, halo, 5, at_chip(side, 0, z, 1))]
+    for n in range(2):
+        parts.append(remote(at_rows(ext, 0, other_half + H * n, H), quarter_in, halo, 6 + n, at_chip(idle_side, 0, z, n)))
+    half_in = remote(relay_in, relay_in, halo, 5, target)
+    half_on = remote(relay_in, at_rows(ext, 4, jnp.where(x == 3, 0, W), W), halo, 8, target)
+    quarter = remote(quarter_in, quarter_in, halo, 6 + core, target)
+    quarter_on = remote(quarter_in, at_rows(ext, 4, jnp.where(x == 1, W, 0) + H * core, H), halo, 9 + core, target)
+    got = [remote(relay_in, area(ext, 4, 0, W), halo, 8, target)]
+    got += [remote(quarter_in, area(ext, 4, 0, H), halo, 9 + n, target) for n in range(2)]
 
     lanes[0].wait()
     lanes[1].wait()
-    when(past_seam, *[copy.start for copy in parts])
+    when(past_seam, parts[1].start, parts[2].start, parts[0].start)
     when(past_seam & has_up, seam_corner.start)
     when(has_up, rows_l.start)
     when(sends_left, cols.start)
@@ -565,13 +582,15 @@
         amps_out[k] = dot(high, chosen) + dot(mid, chosen) + dot(low, chosen)
         return 0
 
-    lax.fori_loop(0, amps.shape[0], reorder_slot, 0)
-    when(is_relay, arrived.wait_recv, passed.start)
+    lax.fori_loop(0, amps.shape[0] // 2, reorder_slot, 0)
+    when(relays_quarter, quarter.wait_recv, quarter_on.start)
+    when(relays_half, half_in.wait_recv, half_on.start)
+    lax.fori_loop(amps.shape[0] // 2, amps.shape[0], reorder_slot, 0)
     when(has_down, rows_l.wait_recv)
     when(has_down & sends_left, on_left.start)
     when(has_down, rows_r.wait_recv)
     when(gets_right, cols.wait_recv)
-    when(at_seam, *[copy.wait_recv for copy in got], parts[3].wait_recv)
+    when(at_seam, *[copy.wait_recv for copy in got])
     when(gets_right & has_down, on_left.wait_recv)
     when(at_seam & has_down, seam_corner.wait_recv)
     when(sends_left, cols.wait_send)
@@ -579,7 +598,8 @@
     when(has_down & sends_left, on_left.wait_send)
     when(past_seam, *[copy.wait_send for copy in parts])
     when(past_seam & has_up, seam_corner.wait_send)
-    when(is_relay, passed.wait_send)
+    when(relays_quarter, quarter_on.wait_send)
+    when(relays_half, half_on.wait_send)
 
 
 def ahead(tile, amps):
@@ -592,14 +612,14 @@
         in_specs=[hbm, hbm],
         out_specs=(vmem, vmem),
         scratch_shapes=[
-            VMEM((2, 2, H, H), F32), VMEM((amps.shape[0], 2, W, H), F32),
-            dma((12,)), dma((12,)), dma((T // H,)), dma((2,)),
+            VMEM((2, 2, W, H), F32), VMEM((amps.shape[0], 2, W, H), F32),
+            dma((11,)), dma((11,)), dma((T // H,)), dma((2,)),
         ],
         compiler_params=pltpu.CompilerParams(
             collective_id=0, has_side_effects=True, vmem_limit_bytes=24 * MIB
         ),
         name="ahead",
-    )(tile, amps)
+    )(pltpu.with_memory_space_constraint(tile, pltpu.HBM), pltpu.with_memory_space_constraint(amps, pltpu.HBM))
 
 
 def on_device(object_tile, probe, amplitudes, positions, counts):

time: 110 us -> 101 us (0.918)
  the two profiles are of different devices: /device:TPU:61 before, /device:TPU:31 now
where the time goes in v5:
time: 101 us; the launch traced here: 100 us
  Pallas kernels  97.6 us (97%)
  local copies, waits for them, and re-layouts  2.13 us (2%)
    pallas_call x1, Pallas kernels, back(): pl.pallas_call(back_kernel, out_shape=(jax.ShapeDtypeStruct((2, T, T), F3...  65.1 us
    pallas_call x1, Pallas kernels, ahead(): pl.pallas_call(ahead_kernel, out_shape=(jax.ShapeDtypeStruct(EXT, F32), j...  26.4 us
    pallas_call x1, Pallas kernels, run_slots(): pl.pallas_call(slots_kernel, out_shape=(jax.ShapeDtypeStruct(EXT, F32), j...  6.1 us
    unnamed x10, local copies, waits for them, and re-layouts  2.13 us

profile of v5, /device:TPU:31, one launch (start us, length us, event | category | flops | bytes accessed | tf_op | source)
XLA Modules:
  0.0 100.5 jit_solution(8199325116857594851)
XLA Ops:
  0.6 0.0 copy-start
  0.6 0.0 copy-start.3
  0.7 0.0 copy-start.2
  0.7 0.0 copy-start.1
  0.7 26.4 %ahead.1 = (f32[2,6,768,128]{3,2,1,0:T(8,128)S(1)}, f32[16,256,256]{2,1,0:T(8,128)S(1)}) custom-call(f32[2,512,512]{2,1,0:T(8,128)} %tile.1, f32[16,256,256]{2,1,0:T(8,128)} %bitcast.5), custom_call_target="tpu_custom_call" | custom-call | tf_op jit(solution)/shard_map/ahead/pallas_call | solution.py:609
  27.1 0.0 copy-done
  27.1 0.0 copy-done.3
  27.1 0.0 copy-done.2
  27.2 0.0 copy-done.1
  27.2 6.1 %slots.1 = (f32[2,6,768,128]{3,2,1,0:T(8,128)S(1)}, f32[4,256,128]{2,1,0:T(8,128)S(1)}) custom-call(s32[2,16]{1,0:T(2,128)S(1)} %bitcast.4, s32[1,16]{1,0:T(1,128)S(1)} %copy-done.3, f32[2,6,768,128]{3,2,1,0:T(8,128)S(1)} %get-tuple-element.6.ext, f32[16,256,256]{2,1,0:T(8,128)S(1)} %get-tuple-element.7.amps, f32[2,256,256]{2,1,0:T(8,128)S(1)} %copy-done.1, ...), custom_call_target="tpu_custom_call" | custom-call | tf_op jit(solution)/shard_map/slots/pallas_call | solution.py:213
  33.3 65.1 %back.1 = (f32[2,512,512]{2,1,0:T(8,128)S(1)}, f32[2,256,256]{2,1,0:T(8,128)S(1)}) custom-call(f32[2,6,768,128]{3,2,1,0:T(8,128)S(1)} %get-tuple-element.8.gext, f32[4,256,128]{2,1,0:T(8,128)S(1)} %get-tuple-element.9.part), custom_call_target="tpu_custom_call" | custom-call | tf_op jit(solution)/shard_map/back/pallas_call | solution.py:476
  98.3 1.3 %copy.10 = f32[2,512,512]{2,1,0:T(8,128)} copy(f32[2,512,512]{2,1,0:T(8,128)S(1)} %get-tuple-element.12) | data formatting | bytes 4194304
  99.7 0.8 copy.11
Async XLA Ops:
  0.6 26.5 %copy-start = (f32[4,256,256]{2,1,0:T(8,128)S(1)}, f32[4,256,256]{2,1,0:T(8,128)}, u32[]{:S(2)}) copy-start(f32[4,256,256]{2,1,0:T(8,128)} %constant.2.clone.table) | copy-start | bytes 3145732
  0.6 26.5 %copy-start.3 = (s32[1,16]{1,0:T(1,128)S(1)}, s32[1,16]{1,0:T(1,128)}, u32[]{:S(2)}) copy-start(s32[1,16]{1,0:T(1,128)} %counts.1) | copy-start | bytes 196
  0.7 26.5 %copy-start.2 = (s32[1,1,16,2]{2,3,1,0:T(2,128)S(1)}, s32[1,1,16,2]{2,3,1,0:T(2,128)}, u32[]{:S(2)}) copy-start(s32[1,1,16,2]{2,3,1,0:T(2,128)} %param.9) | copy-start | bytes 388
  0.7 26.5 %copy-start.1 = (f32[2,256,256]{2,1,0:T(8,128)S(1)}, f32[2,256,256]{2,1,0:T(8,128)}, u32[]{:S(2)}) copy-start(f32[2,256,256]{2,1,0:T(8,128)} %probe.1) | copy-start | bytes 1572868

commit v6 on v5

--- a/solution.py
+++ b/solution.py
@@ -406,12 +406,13 @@
     when(relays_quarter, quarter.wait_recv, quarter_on.start)
     spread = [remote(full.at[own], full.at[own], (x_send, x_recv), 6 + q, far_id(q)) for q in range(1, 8)]
     start(spread)
+    when(has_down, pieces_l[0].start)
     wait(spread)
     own1 = block(base1, 64)
     spread = [remote(full.at[own1], full.at[own1], (p_send, p_recv), 6 + q, near_id(q)) for q in range(1, 8)]
     start(spread)
     when(relays_half, half_in.wait_recv, half_on.start)
-    when(has_down, *[copy.start for copy in pieces_r[1:] + pieces_l])
+    when(has_down, *[copy.start for copy in pieces_l[1:]])
     when(sends_right, cols2.start)
     for n in range(T // H):
         out[:, :, pl.ds(n * H, H)] = gext[:, n, pl.ds(0, T), :]
@@ -465,8 +466,8 @@
     when(relays_half, half_on.wait_send)
 
 
-PIECES_R = (128, 128)
-PIECES_L = (256,)
+PIECES_R = (256,)
+PIECES_L = (64, 192)
 
 
 def back(gext, part):

time: 101 us -> 98.2 us (0.972)
  the two profiles are of different devices: /device:TPU:31 before, /device:TPU:1 now
where the time goes in v6:
time: 98.2 us; the launch traced here: 97.2 us
  Pallas kernels  94.4 us (96%)
  local copies, waits for them, and re-layouts  2.13 us (2%)
    pallas_call x1, Pallas kernels, back(): pl.pallas_call(back_kernel, out_shape=(jax.ShapeDtypeStruct((2, T, T), F3...  61.5 us
    pallas_call x1, Pallas kernels, ahead(): pl.pallas_call(ahead_kernel, out_shape=(jax.ShapeDtypeStruct(EXT, F32), j...  26.8 us
    pallas_call x1, Pallas kernels, run_slots(): pl.pallas_call(slots_kernel, out_shape=(jax.ShapeDtypeStruct(EXT, F32), j...  6.08 us
    unnamed x10, local copies, waits for them, and re-layouts  2.13 us

profile of v6, /device:TPU:1, one launch (start us, length us, event | category | flops | bytes accessed | tf_op | source)
XLA Modules:
  0.0 97.2 jit_solution(18306116810955480726)
XLA Ops:
  0.6 0.0 copy-start
  0.6 0.0 copy-start.3
  0.7 0.0 copy-start.2
  0.7 0.0 copy-start.1
  0.7 26.8 %ahead.1 = (f32[2,6,768,128]{3,2,1,0:T(8,128)S(1)}, f32[16,256,256]{2,1,0:T(8,128)S(1)}) custom-call(f32[2,512,512]{2,1,0:T(8,128)} %tile.1, f32[16,256,256]{2,1,0:T(8,128)} %bitcast.5), custom_call_target="tpu_custom_call" | custom-call | tf_op jit(solution)/shard_map/ahead/pallas_call | solution.py:610
  27.5 0.0 copy-done
  27.5 0.0 copy-done.3
  27.5 0.0 copy-done.2
  27.5 0.0 copy-done.1
  27.5 6.1 %slots.1 = (f32[2,6,768,128]{3,2,1,0:T(8,128)S(1)}, f32[4,256,128]{2,1,0:T(8,128)S(1)}) custom-call(s32[2,16]{1,0:T(2,128)S(1)} %bitcast.4, s32[1,16]{1,0:T(1,128)S(1)} %copy-done.3, f32[2,6,768,128]{3,2,1,0:T(8,128)S(1)} %get-tuple-element.6.ext, f32[16,256,256]{2,1,0:T(8,128)S(1)} %get-tuple-element.7.amps, f32[2,256,256]{2,1,0:T(8,128)S(1)} %copy-done.1, ...), custom_call_target="tpu_custom_call" | custom-call | tf_op jit(solution)/shard_map/slots/pallas_call | solution.py:213
  33.6 61.5 %back.1 = (f32[2,512,512]{2,1,0:T(8,128)S(1)}, f32[2,256,256]{2,1,0:T(8,128)S(1)}) custom-call(f32[2,6,768,128]{3,2,1,0:T(8,128)S(1)} %get-tuple-element.8.gext, f32[4,256,128]{2,1,0:T(8,128)S(1)} %get-tuple-element.9.part), custom_call_target="tpu_custom_call" | custom-call | tf_op jit(solution)/shard_map/back/pallas_call | solution.py:477
  95.1 1.3 %copy.10 = f32[2,512,512]{2,1,0:T(8,128)} copy(f32[2,512,512]{2,1,0:T(8,128)S(1)} %get-tuple-element.12) | data formatting | bytes 4194304
  96.4 0.8 copy.11
Async XLA Ops:
  0.6 26.9 %copy-start = (f32[4,256,256]{2,1,0:T(8,128)S(1)}, f32[4,256,256]{2,1,0:T(8,128)}, u32[]{:S(2)}) copy-start(f32[4,256,256]{2,1,0:T(8,128)} %constant.2.clone.table) | copy-start | bytes 3145732
  0.6 26.8 %copy-start.3 = (s32[1,16]{1,0:T(1,128)S(1)}, s32[1,16]{1,0:T(1,128)}, u32[]{:S(2)}) copy-start(s32[1,16]{1,0:T(1,128)} %counts.1) | copy-start | bytes 196
  0.7 26.8 %copy-start.2 = (s32[1,1,16,2]{2,3,1,0:T(2,128)S(1)}, s32[1,1,16,2]{2,3,1,0:T(2,128)}, u32[]{:S(2)}) copy-start(s32[1,1,16,2]{2,3,1,0:T(2,128)} %param.9) | copy-start | bytes 388
  0.7 26.8 %copy-start.1 = (f32[2,256,256]{2,1,0:T(8,128)S(1)}, f32[2,256,256]{2,1,0:T(8,128)}, u32[]{:S(2)}) copy-start(f32[2,256,256]{2,1,0:T(8,128)} %probe.1) | copy-start | bytes 1572868

commit v7 on v6

--- a/solution.py
+++ b/solution.py
@@ -51,11 +51,13 @@
 
 
 def by_right(x, t, n):
-    return dot(x[0], t[n, 0]) + dot(x[1], t[n, 0]) + dot(x[0], t[n, 1])
+    both = dot(x[...].reshape(2 * W, W), t[n, 0])
+    return both[:W] + both[W:] + dot(x[0], t[n, 1])
 
 
 def by_left(x, t, n):
-    return dot(t[n, 0], x[0]) + dot(t[n, 0], x[1]) + dot(t[n, 1], x[0])
+    both = dot(t[n].reshape(2 * W, W), x[0])
+    return both[:W] + both[W:] + dot(t[n, 0], x[1])
 
 
 def slot_steps(r, c, live, ext, gext, probe, amp, t, win, xe, xo, ye, yo, pgrad):

time: 98.2 us -> 97.3 us (level)
    pallas_call x1, Pallas kernels: 61.5 us -> 56.9 us  [back(): pl.pallas_call(back_kernel, out_shape=(jax.ShapeDtypeStruct((2, T, T), F3...]
    pallas_call x1, Pallas kernels: 6.08 us -> 10.6 us  [run_slots(): pl.pallas_call(slots_kernel, out_shape=(jax.ShapeDtypeStruct(EXT, F32), j...]
where the time goes in v7:
time: 97.3 us; the launch traced here: 97.2 us
  Pallas kernels  94.3 us (97%)
  local copies, waits for them, and re-layouts  2.13 us (2%)
    pallas_call x1, Pallas kernels, back(): pl.pallas_call(back_kernel, out_shape=(jax.ShapeDtypeStruct((2, T, T), F3...  56.9 us
    pallas_call x1, Pallas kernels, ahead(): pl.pallas_call(ahead_kernel, out_shape=(jax.ShapeDtypeStruct(EXT, F32), j...  26.8 us
    pallas_call x1, Pallas kernels, run_slots(): pl.pallas_call(slots_kernel, out_shape=(jax.ShapeDtypeStruct(EXT, F32), j...  10.6 us
    unnamed x10, local copies, waits for them, and re-layouts  2.13 us

profile of v7, /device:TPU:1, one launch (start us, length us, event | category | flops | bytes accessed | tf_op | source)
XLA Modules:
  0.0 97.2 jit_solution(3715299285419083699)
XLA Ops:
  0.6 0.0 copy-start
  0.6 0.0 copy-start.3
  0.7 0.0 copy-start.2
  0.7 0.0 copy-start.1
  0.7 26.8 %ahead.1 = (f32[2,6,768,128]{3,2,1,0:T(8,128)S(1)}, f32[16,256,256]{2,1,0:T(8,128)S(1)}) custom-call(f32[2,512,512]{2,1,0:T(8,128)} %tile.1, f32[16,256,256]{2,1,0:T(8,128)} %bitcast.5), custom_call_target="tpu_custom_call" | custom-call | tf_op jit(solution)/shard_map/ahead/pallas_call | solution.py:612
  27.5 0.0 copy-done
  27.5 0.0 copy-done.3
  27.5 0.0 copy-done.2
  27.5 0.0 copy-done.1
  27.5 10.6 %slots.1 = (f32[2,6,768,128]{3,2,1,0:T(8,128)S(1)}, f32[4,256,128]{2,1,0:T(8,128)S(1)}) custom-call(s32[2,16]{1,0:T(2,128)S(1)} %bitcast.4, s32[1,16]{1,0:T(1,128)S(1)} %copy-done.3, f32[2,6,768,128]{3,2,1,0:T(8,128)S(1)} %get-tuple-element.6.ext, f32[16,256,256]{2,1,0:T(8,128)S(1)} %get-tuple-element.7.amps, f32[2,256,256]{2,1,0:T(8,128)S(1)} %copy-done.1, ...), custom_call_target="tpu_custom_call" | custom-call | tf_op jit(solution)/shard_map/slots/pallas_call | solution.py:215
  38.2 56.9 %back.1 = (f32[2,512,512]{2,1,0:T(8,128)S(1)}, f32[2,256,256]{2,1,0:T(8,128)S(1)}) custom-call(f32[2,6,768,128]{3,2,1,0:T(8,128)S(1)} %get-tuple-element.8.gext, f32[4,256,128]{2,1,0:T(8,128)S(1)} %get-tuple-element.9.part), custom_call_target="tpu_custom_call" | custom-call | tf_op jit(solution)/shard_map/back/pallas_call | solution.py:479
  95.1 1.3 %copy.10 = f32[2,512,512]{2,1,0:T(8,128)} copy(f32[2,512,512]{2,1,0:T(8,128)S(1)} %get-tuple-element.12) | data formatting | bytes 4194304
  96.4 0.8 copy.11
Async XLA Ops:
  0.6 26.9 %copy-start = (f32[4,256,256]{2,1,0:T(8,128)S(1)}, f32[4,256,256]{2,1,0:T(8,128)}, u32[]{:S(2)}) copy-start(f32[4,256,256]{2,1,0:T(8,128)} %constant.2.clone.table) | copy-start | bytes 3145732
  0.6 26.8 %copy-start.3 = (s32[1,16]{1,0:T(1,128)S(1)}, s32[1,16]{1,0:T(1,128)}, u32[]{:S(2)}) copy-start(s32[1,16]{1,0:T(1,128)} %counts.1) | copy-start | bytes 196
  0.7 26.8 %copy-start.2 = (s32[1,1,16,2]{2,3,1,0:T(2,128)S(1)}, s32[1,1,16,2]{2,3,1,0:T(2,128)}, u32[]{:S(2)}) copy-start(s32[1,1,16,2]{2,3,1,0:T(2,128)} %param.9) | copy-start | bytes 388
  0.7 26.8 %copy-start.1 = (f32[2,256,256]{2,1,0:T(8,128)S(1)}, f32[2,256,256]{2,1,0:T(8,128)}, u32[]{:S(2)}) copy-start(f32[2,256,256]{2,1,0:T(8,128)} %probe.1) | copy-start | bytes 1572868

commit v8 on v7

--- a/solution.py
+++ b/solution.py
@@ -469,7 +469,7 @@
 
 
 PIECES_R = (256,)
-PIECES_L = (64, 192)
+PIECES_L = (128, 128)
 
 
 def back(gext, part):

time: 97.3 us -> 98.5 us (1.012)
  Pallas kernels: 94.3 us -> 95.3 us
    pallas_call x1, Pallas kernels: 56.9 us -> 67.4 us  [back(): pl.pallas_call(back_kernel, out_shape=(jax.ShapeDtypeStruct((2, T, T), F3...]
    pallas_call x1, Pallas kernels: 10.6 us -> 1.09 us  [run_slots(): pl.pallas_call(slots_kernel, out_shape=(jax.ShapeDtypeStruct(EXT, F32), j...]
where the time goes in v8:
time: 98.5 us; the launch traced here: 98.1 us
  Pallas kernels  95.3 us (97%)
  local copies, waits for them, and re-layouts  2.13 us (2%)
    pallas_call x1, Pallas kernels, back(): pl.pallas_call(back_kernel, out_shape=(jax.ShapeDtypeStruct((2, T, T), F3...  67.4 us
    pallas_call x1, Pallas kernels, ahead(): pl.pallas_call(ahead_kernel, out_shape=(jax.ShapeDtypeStruct(EXT, F32), j...  26.8 us
    unnamed x10, local copies, waits for them, and re-layouts  2.13 us

profile of v8, /device:TPU:1, one launch (start us, length us, event | category | flops | bytes accessed | tf_op | source)
XLA Modules:
  0.0 98.1 jit_solution(7093814555093997312)
XLA Ops:
  0.6 0.0 copy-start
  0.6 0.0 copy-start.3
  0.7 0.0 copy-start.2
  0.7 0.0 copy-start.1
  0.7 26.8 %ahead.1 = (f32[2,6,768,128]{3,2,1,0:T(8,128)S(1)}, f32[16,256,256]{2,1,0:T(8,128)S(1)}) custom-call(f32[2,512,512]{2,1,0:T(8,128)} %tile.1, f32[16,256,256]{2,1,0:T(8,128)} %bitcast.5), custom_call_target="tpu_custom_call" | custom-call | tf_op jit(solution)/shard_map/ahead/pallas_call | solution.py:612
  27.5 0.0 copy-done
  27.5 0.0 copy-done.3
  27.5 0.0 copy-done.2
  27.5 0.0 copy-done.1
  27.5 1.1 %slots.1 = (f32[2,6,768,128]{3,2,1,0:T(8,128)S(1)}, f32[4,256,128]{2,1,0:T(8,128)S(1)}) custom-call(s32[2,16]{1,0:T(2,128)S(1)} %bitcast.4, s32[1,16]{1,0:T(1,128)S(1)} %copy-done.3, f32[2,6,768,128]{3,2,1,0:T(8,128)S(1)} %get-tuple-element.6.ext, f32[16,256,256]{2,1,0:T(8,128)S(1)} %get-tuple-element.7.amps, f32[2,256,256]{2,1,0:T(8,128)S(1)} %copy-done.1, ...), custom_call_target="tpu_custom_call" | custom-call | tf_op jit(solution)/shard_map/slots/pallas_call | solution.py:215
  28.6 67.4 %back.1 = (f32[2,512,512]{2,1,0:T(8,128)S(1)}, f32[2,256,256]{2,1,0:T(8,128)S(1)}) custom-call(f32[2,6,768,128]{3,2,1,0:T(8,128)S(1)} %get-tuple-element.8.gext, f32[4,256,128]{2,1,0:T(8,128)S(1)} %get-tuple-element.9.part), custom_call_target="tpu_custom_call" | custom-call | tf_op jit(solution)/shard_map/back/pallas_call | solution.py:479
  96.0 1.3 %copy.10 = f32[2,512,512]{2,1,0:T(8,128)} copy(f32[2,512,512]{2,1,0:T(8,128)S(1)} %get-tuple-element.12) | data formatting | bytes 4194304
  97.4 0.8 copy.11
Async XLA Ops:
  0.6 26.9 %copy-start = (f32[4,256,256]{2,1,0:T(8,128)S(1)}, f32[4,256,256]{2,1,0:T(8,128)}, u32[]{:S(2)}) copy-start(f32[4,256,256]{2,1,0:T(8,128)} %constant.2.clone.table) | copy-start | bytes 3145732
  0.6 26.8 %copy-start.3 = (s32[1,16]{1,0:T(1,128)S(1)}, s32[1,16]{1,0:T(1,128)}, u32[]{:S(2)}) copy-start(s32[1,16]{1,0:T(1,128)} %counts.1) | copy-start | bytes 196
  0.7 26.8 %copy-start.2 = (s32[1,1,16,2]{2,3,1,0:T(2,128)S(1)}, s32[1,1,16,2]{2,3,1,0:T(2,128)}, u32[]{:S(2)}) copy-start(s32[1,1,16,2]{2,3,1,0:T(2,128)} %param.9) | copy-start | bytes 388
  0.7 26.8 %copy-start.1 = (f32[2,256,256]{2,1,0:T(8,128)S(1)}, f32[2,256,256]{2,1,0:T(8,128)}, u32[]{:S(2)}) copy-start(f32[2,256,256]{2,1,0:T(8,128)} %probe.1) | copy-start | bytes 1572868
